TPU v7x, 32 devices: a whole 2x2x4 slice. The times are simulated.
32 devices in a mesh: groups: 2 (over y), segment: 8 (over z, x), template: 2 (over core).
Axes of the slice: x: 2, y: 2, z: 4, core: 2. Of those that a mesh axis runs over, the one named last changes fastest.
Arguments:
- strain_frames: bfloat16 [64, 16384], P('segment'), may hold values from -6 to 6
- frame_slot: int32 [8, 8], replicated, may hold values from 0 to 7, as said below
- templates: bfloat16 [4, 2, 131072], P(('groups', 'template'), None, 'segment'), parts along dimension 0, may hold values from -6 to 6
- bin_edges: int32 [4, 3], P(('groups', 'template')), parts along dimension 0, may hold values from 16384 to 114687, as said below
Outputs:
- snr_series: bfloat16 [8, 4, 131072], P('segment', ('groups', 'template')), parts along dimension 1
- chisq_series: bfloat16 [8, 4, 131072], P('segment', ('groups', 'template')), parts along dimension 1
- peak_newsnr: float32 [8, 4], P('segment', ('groups', 'template')), parts along dimension 1
There are 2 independent parts, one for each index of `groups`. A program takes and returns all parts, laid end to end along the dimension named above; an argument that names none is the same for every part. Nothing has to cross between parts.
Inputs may be any that keep to these rules, and one draw needn't show every extreme that they name: Each column frame_slot[:, j] is a permutation of 0 to 7. `bin_edges`: edge number e of a template lies in [(2 e + 1) * 16384, (2 e + 3) * 16384), so the edges rise.
All inputs are finite; a program needn't handle non-finite values.
Results may differ from a plain program's by a relative error of at most 0.011.
Values may be sent and summed in bfloat16 or wider, within the bound.
A program may use at most 64 MiB of HBM per device.

v0:
```python
import math

import jax
import jax.numpy as jnp
from jax import lax
from jax.sharding import PartitionSpec as P

RADIX_A = 64
RADIX_B = 32
RADIX_C = 128


def dft_table(length, orient):
    counter = jnp.arange(length, dtype=jnp.int32)
    product = counter[:, None] * counter[None, :] % length
    angles = orient * 2.0 * math.pi / length * product.astype(jnp.float32)
    cosine = jnp.cos(angles)
    sine = jnp.sin(angles)
    upper = jnp.stack([cosine, -sine], axis=1)
    lower = jnp.stack([sine, cosine], axis=1)
    return jnp.stack([upper, lower], axis=0).astype(jnp.bfloat16)


def rotate(values, phase_index, modulus, orient):
    angles = orient * 2.0 * math.pi / modulus * (phase_index % modulus).astype(jnp.float32)
    cosine = jnp.cos(angles)
    sine = jnp.sin(angles)
    real_part = values[0] * cosine - values[1] * sine
    imag_part = values[0] * sine + values[1] * cosine
    return jnp.stack([real_part, imag_part]).astype(jnp.bfloat16)


def later_passes(level_one, orient, table_three):
    length = RADIX_A * RADIX_B * RADIX_C
    inner = RADIX_B * RADIX_C
    grid_one = (
        jnp.arange(RADIX_A, dtype=jnp.int32)[:, None] * jnp.arange(inner, dtype=jnp.int32)[None, :]
    )
    turned = rotate(level_one, grid_one, length, orient).reshape(2, RADIX_A, RADIX_B, RADIX_C)
    level_two = jnp.einsum(
        "cjdp,dkpr->ckjr", dft_table(RADIX_B, orient), turned, preferred_element_type=jnp.float32
    )
    grid_two = (
        jnp.arange(RADIX_B, dtype=jnp.int32)[:, None]
        * jnp.arange(RADIX_C, dtype=jnp.int32)[None, :]
    )
    turned_two = rotate(level_two, grid_two, inner, orient)
    level_three = jnp.einsum(
        "cldr,dkjr->ckjl", table_three, turned_two, preferred_element_type=jnp.float32
    )
    rows = table_three.shape[1]
    return jnp.transpose(level_three, (0, 3, 2, 1)).reshape(2, rows * inner * RADIX_A // RADIX_C)


def forward_spectrum(real_signal):
    inner = RADIX_B * RADIX_C
    start = real_signal.reshape(RADIX_A, inner)
    table_one = dft_table(RADIX_A, -1.0)[:, :, 0, :]
    level_one = jnp.einsum("ckp,pq->ckq", table_one, start, preferred_element_type=jnp.float32)
    table_three = dft_table(RADIX_C, -1.0)[:, : RADIX_C // 2]
    return later_passes(level_one, -1.0, table_three)


def inverse_kept(masked):
    inner = RADIX_B * RADIX_C
    start = masked.reshape(2, RADIX_A // 2, inner)
    table_one = dft_table(RADIX_A, 1.0)[:, :, :, : RADIX_A // 2]
    level_one = jnp.einsum("ckdp,dpq->ckq", table_one, start, preferred_element_type=jnp.float32)
    table_three = dft_table(RADIX_C, 1.0)[:, RADIX_C // 4 : RADIX_C // 4 + RADIX_C // 2]
    return later_passes(level_one, 1.0, table_three)


def filter_template(spectrum, template, edges):
    length = RADIX_A * RADIX_B * RADIX_C
    kept = length // 2
    temp_real = template[0].astype(jnp.float32)
    temp_imag = template[1].astype(jnp.float32)
    corr_real = spectrum[0] * temp_real + spectrum[1] * temp_imag
    corr_imag = spectrum[1] * temp_real - spectrum[0] * temp_imag
    power = temp_real * temp_real + temp_imag * temp_imag
    total = jnp.sum(power)
    bin_index = jnp.arange(kept, dtype=jnp.int32)
    label = (
        (bin_index >= edges[0]).astype(jnp.int32)
        + (bin_index >= edges[1]).astype(jnp.int32)
        + (bin_index >= edges[2]).astype(jnp.int32)
    )
    pieces = []
    shares = []
    for number in range(4):
        inside = (label == number).astype(jnp.float32)
        shares.append(jnp.sum(power * inside) / total)
        masked = jnp.stack([corr_real * inside, corr_imag * inside]).astype(jnp.bfloat16)
        pieces.append(inverse_kept(masked) / length)
    summed = pieces[0] + pieces[1] + pieces[2] + pieces[3]
    scale = length / total
    snr = jnp.sqrt((summed[0] * summed[0] + summed[1] * summed[1]) * scale)
    chisq = jnp.zeros_like(snr)
    for number in range(4):
        diff_real = pieces[number][0] - shares[number] * summed[0]
        diff_imag = pieces[number][1] - shares[number] * summed[1]
        chisq = chisq + diff_real * diff_real + diff_imag * diff_imag
    chisq = chisq * scale
    reduced = chisq / 6.0
    weighted = snr * ((1.0 + reduced * reduced * reduced) / 2.0) ** (-1.0 / 6.0)
    newsnr = jnp.where(reduced > 1.0, weighted, snr)
    return (snr.astype(jnp.bfloat16), chisq.astype(jnp.bfloat16), jnp.max(newsnr))


def local(strain_frames, frame_slot, templates, bin_edges):
    segments_count = lax.axis_size("segment")
    position = lax.axis_index("segment")
    frame_length = strain_frames.shape[1]
    length = RADIX_A * RADIX_B * RADIX_C
    kept = length // 2
    counter = jnp.arange(segments_count, dtype=jnp.int32)
    slot_now = lax.dynamic_slice_in_dim(frame_slot, position, 1, 1)[:, 0]
    next_index = jnp.minimum(position + 1, segments_count - 1)
    slot_next = lax.dynamic_slice_in_dim(frame_slot, next_index, 1, 1)[:, 0]

    def arrange(slots, frames):
        selector = (counter[:, None] == slots[None, :]).astype(jnp.bfloat16)
        return (
            jnp.dot(selector, frames, preferred_element_type=jnp.float32)
            .astype(jnp.bfloat16)
            .reshape(kept)
        )

    following_rows = jnp.concatenate(
        [strain_frames[1:], jnp.zeros((1, frame_length), jnp.bfloat16)], axis=0
    )
    outgoing = jnp.stack([strain_frames, following_rows], axis=1)
    received = lax.all_to_all(outgoing, "segment", split_axis=0, concat_axis=0, tiled=True)
    leading = arrange(slot_now, received[:, 0])
    trailing = arrange(slot_next, received[:, 1])
    segment_data = jnp.concatenate([leading, trailing])
    whole_templates = lax.all_gather(templates, "segment", axis=2, tiled=True)
    spectrum = forward_spectrum(segment_data)
    snr_one, chisq_one, peak_one = filter_template(spectrum, whole_templates[0], bin_edges[0])
    snr_rows = [snr_one]
    chisq_rows = [chisq_one]
    peak_rows = [peak_one]
    snr_series = jnp.stack(snr_rows)[None]
    chisq_series = jnp.stack(chisq_rows)[None]
    peak_newsnr = jnp.stack(peak_rows)[None]
    return (snr_series, chisq_series, peak_newsnr)


def solution(mesh):
    in_specs = (
        P("segment", None),
        P(),
        P(("groups", "template"), None, "segment"),
        P(("groups", "template"), None),
    )
    out_specs = (
        P("segment", ("groups", "template"), None),
        P("segment", ("groups", "template"), None),
        P("segment", ("groups", "template")),
    )
    return jax.shard_map(local, mesh=mesh, in_specs=in_specs, out_specs=out_specs, check_vma=False)
```

profile of v0, /device:TPU:0, one launch (start us, length us, event | category | flops | bytes accessed | tf_op | source)
XLA Modules:
  0.0 121.7 jit_solution(296445114597201190)
XLA Ops:
  0.6 1.0 slice.196
  1.7 1.0 pad_maximum_fusion
  2.7 1.3 %copy.65 = bf16[8,2,16384]{2,1,0:T(2,128)(2,1)} copy(bf16[8,2,16384]{2,0,1:T(8,128)(2,1)S(1)} %pad_maximum_fusion) | data formatting | bytes 1048576 | tf_op jit(solution)/shard_map/stack | solution.py:132
  4.1 7.3 %all-to-all-start = ((bf16[8,2,16384]{2,1,0:T(2,128)(2,1)}), bf16[8,2,16384]{2,1,0:T(2,128)(2,1)S(1)}, u32[]{:S(2)}, u32[]{:S(2)}) async-start(bf16[8,2,16384]{2,1,0:T(2,128)(2,1)} %copy.65), calls=%async_computation | async-start | bytes 1048576 | tf_op jit(solution)/shard_map/all_to_all | solution.py:133
  11.9 0.1 fusion.104
  12.0 0.1 cosine_convert_fusion.2
  12.2 0.1 negate_convert_fusion.2
  12.4 0.3 fusion.93
  12.7 0.3 fusion.92
  13.0 0.3 cosine_convert_fusion.1
  13.2 0.3 negate_convert_fusion.1
  13.6 0.2 negate_convert_fusion.3
  13.8 0.6 fusion.140
  14.4 35.5 %all_gather.3 = bf16[1,2,131072]{2,1,0:T(2,128)(2,1)S(1)} all-gather(bf16[1,2,16384]{2,1,0:T(2,128)(2,1)S(1)} %copy-done.3), channel_id=1, replica_groups=mesh['groups'=2,'segment'=8,'template'=2] {'segment'}, dimensions={2}, use_global_device_ids=true | all-gather | bytes 589824 | tf_op jit(solution)/shard_map/all_gather | solution.py:137
  49.9 4.1 %fusion.81 = (f32[131072]{0:T(1024)S(1)}, f32[131072]{0:T(1024)S(1)}, f32[]{:T(128)}, f32[1,1,131072]{2,1,0:T(1,128)S(1)}) fusion(bf16[1,2,131072]{2,1,0:T(2,128)(2,1)S(1)} %all_gather.3), kind=kLoop, calls=%fused_computation.186 | loop fusion | flops 786431 | bytes 2097156 | tf_op jit(solution)/shard_map/convert_element_type | solution.py:76
  54.0 2.9 %select_reduce_fusion.3 = (f32[]{:T(128)}, f32[]{:T(128)}, f32[]{:T(128)}, f32[]{:T(128)}) fusion(f32[131072]{0:T(1024)S(1)} %bitcast.310, s32[]{:T(128)} %bitcast.4, s32[]{:T(128)} %bitcast.3, s32[]{:T(128)} %bitcast.2), kind=kLoop, calls=%fused_computation.155 | loop fusion | flops 2621436 | bytes 524316 | tf_op jit(solution)/shard_map/reduce_sum | solution.py:92
  56.9 0.9 reshape.1209
  63.7 0.9 reshape.1210
  64.6 0.2 dynamic-slice_reduce_fusion.1
  64.9 0.3 negate_convert_fusion
  65.3 0.9 fusion.139
  66.2 0.4 convolution_convert_fusion.1
  66.6 0.2 concatenate.30
  66.8 0.4 convolution_convert_fusion
  67.2 0.2 concatenate.31
  67.5 0.4 fusion.57
  67.9 4.8 %fusion.79 = (bf16[8,8,32,128]{3,1,2,0:T(8,128)(2,1)S(1)}, bf16[8,8,32,128]{3,1,2,0:T(8,128)(2,1)S(1)}) fusion(f32[2,64,4096]{2,1,0:T(8,128)S(1)} %fusion.57), kind=kLoop, calls=%fused_computation.184 | loop fusion | flops 5767168 | bytes 3145728
  72.9 0.5 convolution_bitcast_fusion.9
  73.4 0.3 subtract_convert_fusion.8
  73.7 0.5 convolution_bitcast_fusion.8
  74.1 0.2 fusion.138
  74.3 1.1 copy.71
  75.4 0.4 squeeze.55
  75.8 1.1 copy.70
  76.9 0.4 squeeze.54
  77.3 3.3 %select_convert_fusion.5 = (bf16[1,32,4096]{2,1,0:T(8,128)(2,1)S(1)}, bf16[1,32,4096]{2,1,0:T(8,128)(2,1)S(1)}, bf16[1,32,4096]{2,1,0:T(8,128)(2,1)S(1)}, bf16[1,32,4096]{2,1,0:T(8,128)(2,1)S(1)}) fusion(s32[]{:T(128)} %bitcast.4, s32[]{:T(128)} %bitcast.3, s32[]{:T(128)} %bitcast.2, f32[1,32,4096]{2,1,0:T(8,128)S(1)} %squeeze.55, ...), kind=kLoop, calls=%fused_computation.170 | loop fusion | flops 2752512 | bytes 3145740 | tf_op jit(solution)/shard_map/convert.25
  80.5 2.3 %select_convert_fusion.6 = (bf16[1,32,4096]{2,1,0:T(8,128)(2,1)S(1)}, bf16[1,32,4096]{2,1,0:T(8,128)(2,1)S(1)}, bf16[1,32,4096]{2,1,0:T(8,128)(2,1)S(1)}, bf16[1...) fusion(bf16[1,32,4096]{2,1,0:T(8,128)(2,1)S(1)} %get-tuple-element.42, ...), kind=kLoop, calls=%fused_computation.171 | loop fusion | flops 2490368 | bytes 2097164 | tf_op jit(solution)/shard_map/convert.50
  82.8 0.5 convolution_bitcast_fusion.3
  83.3 4.6 %fusion.49 = (bf16[8,8,32,128]{3,1,2,0:T(8,128)(2,1)S(1)}, bf16[8,8,32,128]{3,1,2,0:T(8,128)(2,1)S(1)}) fusion(f32[2,64,4096]{2,1,0:T(8,128)S(1)} %convolution_bitcast_fusion.3), kind=kLoop, calls=%fused_computation.114 | loop fusion | flops 5767168 | bytes 3145728
  88.2 0.5 convolution_bitcast_fusion.2
  88.6 4.6 %fusion.51 = (bf16[8,8,32,128]{3,1,2,0:T(8,128)(2,1)S(1)}, bf16[8,8,32,128]{3,1,2,0:T(8,128)(2,1)S(1)}) fusion(f32[2,64,4096]{2,1,0:T(8,128)S(1)} %convolution_bitcast_fusion.2), kind=kLoop, calls=%fused_computation.116 | loop fusion | flops 5767168 | bytes 3145728
  93.5 0.5 convolution_bitcast_fusion.1
  94.0 4.6 %fusion.53 = (bf16[8,8,32,128]{3,1,2,0:T(8,128)(2,1)S(1)}, bf16[8,8,32,128]{3,1,2,0:T(8,128)(2,1)S(1)}) fusion(f32[2,64,4096]{2,1,0:T(8,128)S(1)} %convolution_bitcast_fusion.1), kind=kLoop, calls=%fused_computation.118 | loop fusion | flops 5767168 | bytes 3145728
  98.8 0.5 convolution_bitcast_fusion
  99.3 4.8 %fusion.55 = (bf16[8,8,32,128]{3,1,2,0:T(8,128)(2,1)S(1)}, bf16[8,8,32,128]{3,1,2,0:T(8,128)(2,1)S(1)}) fusion(f32[2,64,4096]{2,1,0:T(8,128)S(1)} %convolution_bitcast_fusion), kind=kLoop, calls=%fused_computation.120 | loop fusion | flops 5767168 | bytes 3145728
  104.4 0.5 convolution_bitcast_fusion.7
  104.9 0.5 convolution_bitcast_fusion.6
  105.4 0.5 convolution_bitcast_fusion.5
  105.8 0.5 convolution_bitcast_fusion.4
  106.3 1.3 %subtract_convert_fusion.4 = (bf16[1,64,32,128]{3,2,0,1:T(8,128)(2,1)S(1)}, bf16[1,64,32,128]{3,2,0,1:T(8,128)(2,1)S(1)}, bf16[1,64,32,128]{3,2,0,1:T(8,128)(2,1...) fusion(f32[2,64,32,128]{3,2,0,1:T(8,128)S(1)} %convolution_bitc, ...), kind=kLoop, calls=%fused_computation.90 | loop fusion | flops 8388608 | bytes 12615680 | tf_op jit(solution)/shard_map/convert.19
  107.6 0.5 fusion.2
  108.1 0.4 fusion.1
  108.5 0.5 fusion.3
  109.0 0.5 add_add_fusion
  109.5 2.4 %broadcast_multiply_fusion = (f32[1,64,32,64]{1,2,0,3:T(8,128)S(1)}, bf16[1,64,32,64]{1,2,0,3:T(8,128)(2,1)}, bf16[1,64,32,64]{1,2,0,3:T(8,128)(2,1)}, f32[1,64,32,64]{1,2,0,3:T(8,128)S(1)}) fusion(f32[]{:T(128)S(6)} %div.55, f32[2,64,32,64]{1,2,0,3:T(8,128)S(1)} %get-tuple-element.79, f32[]{:T(128)S(6)} %div.59, f32[2,64,32,64]{1,2,0,3:T(8,128)S(1)} %fusion.1, ...), kind=kLoop, calls=%fused_computation.151 | loop fusion | flops 5111808 | bytes 6815764 | tf_op jit(solution)/shard_map/div | solution.py:104
  112.0 1.1 copy.86
  113.1 1.0 reshape.1304
  114.0 2.1 %copy.85 = bf16[1,64,32,64]{3,2,1,0:T(8,128)(2,1)S(1)} copy(bf16[1,64,32,64]{1,2,0,3:T(8,128)(2,1)} %get-tuple-element.12) | data formatting | bytes 524288 | tf_op jit(solution)/shard_map/convert_element_type | solution.py:107
  116.2 1.1 reshape.1302
  117.3 1.1 copy.84
  118.3 1.1 sqrt.17
  119.4 1.1 copy.87
  120.5 0.2 sqrt.18
  120.7 1.0 fusion.48
  (50 shorter events, 2.3 us)
Async XLA Ops:
  1.6 12.1 %copy-start.5 = (s32[1,3]{1,0:T(1,128)S(1)}, s32[1,3]{1,0:T(1,128)}, u32[]{:S(2)}) copy-start(s32[1,3]{1,0:T(1,128)} %param.7) | copy-start | bytes 40
  1.7 12.7 %copy-start.3 = (bf16[1,2,16384]{2,1,0:T(2,128)(2,1)S(1)}, bf16[1,2,16384]{2,1,0:T(2,128)(2,1)}, u32[]{:S(2)}) copy-start(bf16[1,2,16384]{2,1,0:T(2,128)(2,1)} %param.6) | copy-start | bytes 196612
  4.1 61.2 %all-to-all-start = ((bf16[8,2,16384]{2,1,0:T(2,128)(2,1)}), bf16[8,2,16384]{2,1,0:T(2,128)(2,1)S(1)}, u32[]{:S(2)}, u32[]{:S(2)}) async-start(bf16[8,2,16384]{2,1,0:T(2,128)(2,1)} %copy.65), calls=%async_computation | async-start | bytes 1048576 | tf_op jit(solution)/shard_map/all_to_all | solution.py:133
  49.9 14.7 %copy-start.4 = (s32[8,8]{1,0:T(8,128)S(1)}, s32[8,8]{1,0:T(8,128)}, u32[]{:S(2)}) copy-start(s32[8,8]{1,0:T(8,128)} %param.5) | copy-start | bytes 772
  75.8 1.5 %copy-start = (f32[1,32,4096]{2,1,0:T(8,128)S(1)}, f32[1,32,4096]{2,1,0:T(8,128)}, u32[]{:S(2)}) copy-start(f32[1,32,4096]{2,1,0:T(8,128)} %reshape.1209) | copy-start | bytes 1572868
  113.0 4.2 %copy-start.1 = (bf16[1,64,32,64]{1,2,0,3:T(8,128)(2,1)S(1)}, bf16[1,64,32,64]{1,2,0,3:T(8,128)(2,1)}, u32[]{:S(2)}) copy-start(bf16[1,64,32,64]{1,2,0,3:T(8,128)(2,1)} %get-tuple-element.31) | copy-start | bytes 786436
  119.4 1.3 %copy-start.2 = (f32[131072]{0:T(1024)S(1)}, f32[131072]{0:T(1024)}, u32[]{:S(2)}) copy-start(f32[131072]{0:T(1024)} %reshape.1304) | copy-start | bytes 1572868
where the time goes:
time: 122 us
  other arithmetic  44.6 us (37%)
  blocking collectives  35.5 us (29%)
  local copies, waits for them, and re-layouts  19.4 us (16%)
  matrix products  7.79 us (6%)
  starting transfers between devices  7.25 us (6%)
  between operations  7.15 us (6%)
    all_gather x1, blocking collectives, local(): whole_templates = lax.all_gather(templates, 'segment', axis=2, tiled=True)  35.5 us
    unnamed x5, other arithmetic  23.3 us
    another operation x19, other arithmetic  9.6 us
    all_to_all x1, starting transfers between devices, local(): lax.all_to_all(outgoing, 'segment', split_axis=0, concat_axis=0, tiled=True)  7.25 us
    convert_element_type x1, other arithmetic, filter_template(): temp_real = template[0].astype(jnp.float32)  4.07 us
    convert_element_type x2, local copies, waits for them, and re-layouts, filter_template(): chisq.astype(jnp.bfloat16)  3.2 us
    reduce_sum x1, other arithmetic, filter_template(): shares.append(jnp.sum(power * inside) / total)  2.89 us
  transfers between devices with their start and end apart: 1, of which 0 were waited for; matrix products, arithmetic and copies ran while one was open for 10% of the time, Pallas kernels for 0%

commit v1 on v0

v1 whole, which is shorter than its diff:
```python
import functools
import math

import jax
import jax.numpy as jnp
import numpy as np
from jax import lax
from jax.experimental import pallas as pl
from jax.experimental.pallas import tpu as pltpu
from jax.sharding import PartitionSpec as P

RADIX_A = 64
RADIX_B = 32
RADIX_C = 128
LENGTH = RADIX_A * RADIX_B * RADIX_C
INNER = RADIX_B * RADIX_C
KEPT = LENGTH // 2
SUBROWS = 4
WIDE = INNER // 2
F32 = jnp.float32
BF16 = jnp.bfloat16


def dft_table(length, orient):
    counter = np.arange(length)
    angles = orient * 2.0 * math.pi / length * (counter[:, None] * counter[None, :] % length)
    cosine, sine = np.cos(angles), np.sin(angles)
    upper = np.stack([cosine, -sine], axis=1)
    lower = np.stack([sine, cosine], axis=1)
    return np.stack([upper, lower], axis=0).astype(np.float32)


def tables():
    base = dft_table(RADIX_A, -1.0)[:, :, 0, :]
    first_fwd = np.zeros((SUBROWS, 2, RADIX_A, RADIX_A, SUBROWS), np.float32)
    for sub in range(SUBROWS):
        first_fwd[sub, :, :, :, sub] = base
    first_fwd = first_fwd.reshape(SUBROWS * 2 * RADIX_A, RADIX_A * SUBROWS)
    base = dft_table(RADIX_A, 1.0)[:, :, :, : RADIX_A // 2]
    first_inv = np.zeros((2, 2, RADIX_A, 2, RADIX_A // 2, 2), np.float32)
    for half in range(2):
        first_inv[half, :, :, :, :, half] = base
    first_inv = first_inv.reshape(4 * RADIX_A, 2 * RADIX_A)
    third_fwd = dft_table(RADIX_C, -1.0)[:, : RADIX_C // 2].reshape(RADIX_C, 2 * RADIX_C)
    low = RADIX_C // 4
    third_inv = dft_table(RADIX_C, 1.0)[:, low : low + RADIX_C // 2].reshape(RADIX_C, 2 * RADIX_C)
    third_inv = third_inv.astype(BF16).astype(np.float32) / LENGTH
    k1 = np.arange(RADIX_A)[None, :, None]
    q1 = np.arange(RADIX_B)[:, None, None]
    q2 = np.arange(RADIX_C)[None, None, :]
    angle = 2.0 * math.pi / LENGTH * (k1 * (RADIX_C * q1 + q2) % LENGTH)
    turn_one = np.stack([np.cos(angle), np.sin(angle)]).astype(np.float32)
    angle = 2.0 * math.pi / INNER * (q1 * q2 % INNER)
    turn_two = np.stack([np.cos(angle), np.sin(angle)]).astype(np.float32)
    turn_two = np.broadcast_to(turn_two, (2, RADIX_B, 8, RADIX_C)).copy()
    return (
        first_fwd.astype(BF16),
        first_inv.astype(BF16),
        third_fwd.astype(BF16),
        third_inv.astype(BF16),
        turn_one,
        turn_two,
    )


def cadd(a, b):
    return (a[0] + b[0], a[1] + b[1])


def csub(a, b):
    return (a[0] - b[0], a[1] - b[1])


def quarter(a, orient):
    return (-a[1], a[0]) if orient > 0 else (a[1], -a[0])


def spin(a, eighths, orient):
    eighths = eighths % 32
    if eighths == 0:
        return a
    if eighths == 8:
        return quarter(a, orient)
    if eighths == 4:
        root = math.sqrt(0.5)
        b = quarter(a, orient)
        return ((a[0] + b[0]) * root, (a[1] + b[1]) * root)
    angle = orient * 2.0 * math.pi * eighths / 32
    cosine, sine = math.cos(angle), math.sin(angle)
    return (a[0] * cosine - a[1] * sine, a[0] * sine + a[1] * cosine)


def dft4(x, orient):
    a, b = cadd(x[0], x[2]), csub(x[0], x[2])
    c, d = cadd(x[1], x[3]), quarter(csub(x[1], x[3]), orient)
    return [cadd(a, c), cadd(b, d), csub(a, c), csub(b, d)]


def dft8(x, orient):
    even = dft4(x[0::2], orient)
    odd = dft4(x[1::2], orient)
    odd = [spin(v, 4 * k, orient) for k, v in enumerate(odd)]
    return [cadd(e, o) for e, o in zip(even, odd)] + [csub(e, o) for e, o in zip(even, odd)]


def middle(level_ref, per_row, orient, turn_one_ref, turn_two_ref, turned_ref):
    def turn(value, cosine, sine):
        if orient < 0:
            return (value[0] * cosine + value[1] * sine, value[1] * cosine - value[0] * sine)
        return (value[0] * cosine - value[1] * sine, value[0] * sine + value[1] * cosine)

    def group(g, carry):
        start = pl.multiple_of(g * 8, 8)
        rows = pl.ds(start, 8)

        def load(q1):
            block, lane = q1 // per_row, (q1 % per_row) * RADIX_C
            lanes = slice(lane, lane + RADIX_C)
            real = level_ref[pl.ds(pl.multiple_of(block * 2 * RADIX_A + start, 8), 8), lanes]
            imag = level_ref[
                pl.ds(pl.multiple_of((block * 2 + 1) * RADIX_A + start, 8), 8), lanes
            ]
            return turn((real, imag), turn_one_ref[0, q1, rows, :], turn_one_ref[1, q1, rows, :])

        first = []
        for b in range(8):
            four = dft4([load(8 * a + b) for a in range(4)], orient)
            first.append([spin(v, b * ja, orient) for ja, v in enumerate(four)])
        for ja in range(4):
            eight = dft8([first[b][ja] for b in range(8)], orient)
            for jb in range(8):
                j1 = ja + 4 * jb
                value = turn(eight[jb], turn_two_ref[0, j1], turn_two_ref[1, j1])
                out = pl.ds(pl.multiple_of(j1 * RADIX_A + start, 8), 8)
                turned_ref[out, :RADIX_C] = value[0]
                turned_ref[out, RADIX_C:] = value[1]
        return carry

    lax.fori_loop(0, RADIX_A // 8, group, 0)


def last(table_ref, turned_ref, store):
    step = 512
    for chunk in range(WIDE // step):
        block = turned_ref[chunk * step : (chunk + 1) * step, :].astype(BF16)
        store(
            slice(chunk * step, (chunk + 1) * step),
            lax.dot_general(
                table_ref[...], block, (((1,), (1,)), ((), ())), preferred_element_type=F32
            ),
        )


def compute_kernel(
    edges_ref,
    segment_ref,
    template_ref,
    first_fwd_ref,
    first_inv_ref,
    third_fwd_ref,
    third_inv_ref,
    turn_one_ref,
    turn_two_ref,
    snr_ref,
    chisq_ref,
    peak_ref,
    level_fwd_ref,
    level_inv_ref,
    turned_ref,
    corr_ref,
    piece_ref,
):
    level_fwd_ref[...] = jnp.dot(
        first_fwd_ref[...], segment_ref[...], preferred_element_type=F32
    )
    middle(level_fwd_ref, 8, -1, turn_one_ref, turn_two_ref, turned_ref)

    def keep_spectrum(lanes, value):
        corr_ref[:, lanes] = value

    last(third_fwd_ref, turned_ref, keep_spectrum)
    edges = [edges_ref[0, e] for e in range(3)]
    column = lax.broadcasted_iota(jnp.int32, (8, WIDE), 1)
    row = lax.broadcasted_iota(jnp.int32, (8, WIDE), 0)

    def correlate(s, sums):
        place = pl.multiple_of(s * 8, 8)
        both = template_ref[pl.ds(pl.multiple_of(s * 16, 16), 16), :].astype(F32)
        temp_real, temp_imag = both[:8], both[8:]
        upper = pl.ds(place, 8)
        lower = pl.ds(pl.multiple_of(RADIX_A + place, 8), 8)
        spec_real, spec_imag = corr_ref[upper, :], corr_ref[lower, :]
        corr_ref[upper, :] = spec_real * temp_real + spec_imag * temp_imag
        corr_ref[lower, :] = spec_imag * temp_real - spec_real * temp_imag
        power = temp_real * temp_real + temp_imag * temp_imag
        bins = (row + place) * WIDE + column

        def fold(values):
            return jnp.sum(values.reshape(8, WIDE // RADIX_C, RADIX_C), axis=1)

        above = [fold(jnp.where(bins >= edge, power, 0.0)) for edge in edges]
        parts = [fold(power)] + above
        return tuple(a + b for a, b in zip(sums, parts))

    zero = jnp.zeros((8, RADIX_C), F32)
    sums = lax.fori_loop(0, 8, correlate, (zero,) * 4)
    sums = [jnp.sum(v, axis=(0, 1), keepdims=True) for v in sums]
    total = sums[0]
    shares = [
        (sums[0] - sums[1]) / total,
        (sums[1] - sums[2]) / total,
        (sums[2] - sums[3]) / total,
        sums[3] / total,
    ]
    scale = float(LENGTH) / total

    def one_piece(number, carry):
        low = jnp.where(
            number == 0,
            0,
            jnp.where(number == 1, edges[0], jnp.where(number == 2, edges[1], edges[2])),
        )
        high = jnp.where(
            number == 0,
            edges[0],
            jnp.where(number == 1, edges[1], jnp.where(number == 2, edges[2], KEPT)),
        )
        step = 512
        for chunk in range(WIDE // step):
            lanes = slice(chunk * step, (chunk + 1) * step)
            shape = (2, RADIX_A, step)
            bins = (
                lax.broadcasted_iota(jnp.int32, shape, 1) * WIDE
                + lax.broadcasted_iota(jnp.int32, shape, 2)
                + chunk * step
            ).reshape(2 * RADIX_A, step)
            masked = jnp.where((bins >= low) & (bins < high), corr_ref[:, lanes], 0.0)
            level_inv_ref[:, lanes] = jnp.dot(
                first_inv_ref[...], masked.astype(BF16), preferred_element_type=F32
            )
        middle(level_inv_ref, 16, 1, turn_one_ref, turn_two_ref, turned_ref)

        def keep_piece(lanes, value):
            piece_ref[number, :, lanes] = value

        last(third_inv_ref, turned_ref, keep_piece)
        return carry

    lax.fori_loop(0, 4, one_piece, 0)

    def finish(t, best):
        rows = pl.ds(pl.multiple_of(t * 16, 16), 16)
        lower = pl.ds(pl.multiple_of(RADIX_A + t * 16, 16), 16)
        for chunk in range(WIDE // 512):
            lanes = slice(chunk * 512, (chunk + 1) * 512)
            real = [piece_ref[b, rows, lanes] for b in range(4)]
            imag = [piece_ref[b, lower, lanes] for b in range(4)]
            sum_real = real[0] + real[1] + real[2] + real[3]
            sum_imag = imag[0] + imag[1] + imag[2] + imag[3]
            snr = jnp.sqrt((sum_real * sum_real + sum_imag * sum_imag) * scale)
            chisq = jnp.zeros_like(snr)
            for b in range(4):
                diff_real = real[b] - shares[b] * sum_real
                diff_imag = imag[b] - shares[b] * sum_imag
                chisq = chisq + diff_real * diff_real + diff_imag * diff_imag
            chisq = chisq * scale
            reduced = chisq * (1.0 / 6.0)
            base = (1.0 + reduced * reduced * reduced) * 0.5
            weighted = snr * jnp.exp(jnp.log(base) * (-1.0 / 6.0))
            newsnr = jnp.where(reduced > 1.0, weighted, snr)
            snr_ref[rows, lanes] = snr.astype(BF16)
            chisq_ref[rows, lanes] = chisq.astype(BF16)
            for part in range(4):
                best = jnp.maximum(best, newsnr[:, part * RADIX_C : (part + 1) * RADIX_C])
        return best

    best = lax.fori_loop(0, 4, finish, jnp.zeros((16, RADIX_C), F32))
    peak_ref[...] = jnp.max(best, axis=(0, 1), keepdims=True)


def compute(edges, segment, template):
    vmem = pl.BlockSpec(memory_space=pltpu.VMEM)
    return pl.pallas_call(
        compute_kernel,
        out_shape=(
            jax.ShapeDtypeStruct((RADIX_A, WIDE), BF16),
            jax.ShapeDtypeStruct((RADIX_A, WIDE), BF16),
            jax.ShapeDtypeStruct((1, 1), F32),
        ),
        in_specs=[pl.BlockSpec(memory_space=pltpu.SMEM)] + [vmem] * 8,
        out_specs=(vmem, vmem, vmem),
        scratch_shapes=[
            pltpu.VMEM((SUBROWS * 2 * RADIX_A, INNER // SUBROWS), F32),
            pltpu.VMEM((4 * RADIX_A, WIDE), F32),
            pltpu.VMEM((WIDE, 2 * RADIX_C), F32),
            pltpu.VMEM((2 * RADIX_A, WIDE), F32),
            pltpu.VMEM((4, 2 * RADIX_A, WIDE), F32),
        ],
        compiler_params=pltpu.CompilerParams(vmem_limit_bytes=40 * 1024 * 1024),
    )(edges, segment, template, *[jnp.asarray(t) for t in tables()])


def move_general(strain_frames, frame_slot, templates):
    segments_count = lax.axis_size("segment")
    position = lax.axis_index("segment")
    frame_length = strain_frames.shape[1]
    counter = jnp.arange(segments_count, dtype=jnp.int32)
    slot_now = lax.dynamic_slice_in_dim(frame_slot, position, 1, 1)[:, 0]
    next_index = jnp.minimum(position + 1, segments_count - 1)
    slot_next = lax.dynamic_slice_in_dim(frame_slot, next_index, 1, 1)[:, 0]

    def arrange(slots, frames):
        selector = (counter[:, None] == slots[None, :]).astype(BF16)
        return jnp.dot(selector, frames, preferred_element_type=F32).astype(BF16).reshape(KEPT)

    following_rows = jnp.concatenate(
        [strain_frames[1:], jnp.zeros((1, frame_length), BF16)], axis=0
    )
    outgoing = jnp.stack([strain_frames, following_rows], axis=1)
    received = lax.all_to_all(outgoing, "segment", split_axis=0, concat_axis=0, tiled=True)
    leading = arrange(slot_now, received[:, 0])
    trailing = arrange(slot_next, received[:, 1])
    segment = jnp.concatenate([leading, trailing]).reshape(RADIX_A * SUBROWS, INNER // SUBROWS)
    whole = lax.all_gather(templates, "segment", axis=2, tiled=True)
    template = whole.reshape(2, 8, 8, WIDE).transpose(1, 0, 2, 3).reshape(2 * RADIX_A, WIDE)
    return segment, template


def local(strain_frames, frame_slot, templates, bin_edges):
    segment, template = move_general(strain_frames, frame_slot, templates)
    snr, chisq, peak = compute(bin_edges, segment, template)
    return (snr.reshape(1, 1, KEPT), chisq.reshape(1, 1, KEPT), peak)


def solution(mesh):
    in_specs = (
        P("segment", None),
        P(),
        P(("groups", "template"), None, "segment"),
        P(("groups", "template"), None),
    )
    out_specs = (
        P("segment", ("groups", "template"), None),
        P("segment", ("groups", "template"), None),
        P("segment", ("groups", "template")),
    )
    return jax.shard_map(local, mesh=mesh, in_specs=in_specs, out_specs=out_specs, check_vma=False)
```

time: 122 us -> 76.2 us (0.62)
  other arithmetic: 44.6 us -> 2.07 us
  Pallas kernels: 0 us -> 14.3 us
  local copies, waits for them, and re-layouts: 19.4 us -> 10.9 us
  between operations: 7.15 us -> 0.78 us
  matrix products: 7.79 us -> 1.8 us
  blocking collectives: 35.5 us -> 38.6 us
    unnamed x5 -> x0, other arithmetic: 23.3 us -> none
    pallas_call x0 -> x1, Pallas kernels: none -> 14.3 us  [compute(): pl.pallas_call(compute_kernel, out_shape=(jax.ShapeDtypeStruct((RADIX_A,...]
    another operation x26 -> x1, other arithmetic: 10.7 us -> 1 us  [move_general(): outgoing = jnp.stack([strain_frames, following_rows], axis=1)]
    dot_general x17 -> x2, matrix products: 7.79 us -> 1.8 us  [arrange(): jnp.dot(selector, frames, preferred_element_type=F32).astype(BF16)]
    convert_element_type x4 -> x0, local copies, waits for them, and re-layouts: 4.97 us -> none  [the longest x2 3.2 us: filter_template(): chisq.astype(jnp.bfloat16)]
    convert_element_type x1 -> x0, other arithmetic: 4.07 us -> none  [filter_template(): temp_real = template[0].astype(jnp.float32)]
    reshape x0 -> x3, local copies, waits for them, and re-layouts: none -> 3.31 us  [the longest x2 3.28 us: local(): return (snr.reshape(1, 1, KEPT), chisq.reshape(1, 1, KEPT), peak)]
    all_gather x1, blocking collectives: 35.5 us -> 38.6 us  [move_general(): whole = lax.all_gather(templates, 'segment', axis=2, tiled=True)]
  transfers between devices with their start and end apart: 1 -> 1, of which waited for: 0 -> 0; matrix products, arithmetic and copies ran while one was open for 10% -> 1% of each run, Pallas kernels for 0% -> 0%
where the time goes in v1:
time: 76.2 us; the launch traced here: 75.8 us
  blocking collectives  38.6 us (51%)
  Pallas kernels  14.3 us (19%)
  local copies, waits for them, and re-layouts  10.9 us (14%)
  starting transfers between devices  7.38 us (10%)
  other arithmetic  2.07 us (3%)
  matrix products  1.8 us (2%)
  between operations  0.78 us (1%)
    all_gather x1, blocking collectives, move_general(): whole = lax.all_gather(templates, 'segment', axis=2, tiled=True)  38.6 us
    pallas_call x1, Pallas kernels, compute(): pl.pallas_call(compute_kernel, out_shape=(jax.ShapeDtypeStruct((RADIX_A,...  14.3 us
    all_to_all x1, starting transfers between devices, move_general(): lax.all_to_all(outgoing, 'segment', split_axis=0, concat_axis=0, tiled=True)  7.38 us
    reshape x2, local copies, waits for them, and re-layouts, local(): return (snr.reshape(1, 1, KEPT), chisq.reshape(1, 1, KEPT), peak)  3.28 us
    dot_general x2, matrix products, arrange(): jnp.dot(selector, frames, preferred_element_type=F32).astype(BF16)  1.8 us
    unnamed x21, local copies, waits for them, and re-layouts  1.73 us
    concatenate x2, local copies, waits for them, and re-layouts, move_general(): jnp.concatenate([leading, trailing])  1.66 us
  transfers between devices with their start and end apart: 1, of which 0 were waited for; matrix products, arithmetic and copies ran while one was open for 1% of the time, Pallas kernels for 0%

profile of v1, /device:TPU:0, one launch (start us, length us, event | category | flops | bytes accessed | tf_op | source)
XLA Modules:
  0.0 75.8 jit_solution(12169199891104863888)
XLA Ops:
  0.6 0.0 copy-start.8
  0.6 1.0 %slice.9 = bf16[7,16384]{1,0:T(8,128)(2,1)S(1)} slice(bf16[8,16384]{1,0:T(8,128)(2,1)} %param.10), slice={[1:8], [0:16384]} | slice | bytes 458752 | tf_op jit(solution)/shard_map/slice | solution.py:317
  1.7 1.0 %pad_maximum_fusion = bf16[8,2,16384]{2,0,1:T(8,128)(2,1)S(1)} fusion(bf16[8,1,16384]{2,0,1:T(8,128)(2,1)S(1)} %pad_bitcast_fusion, bf16[8,1,16384]{2,0,1:T(8,128)(2,1)} %bitcast.21), kind=kLoop, calls=%fused_computation.3 | loop fusion | flops 262144 | bytes 1048576 | tf_op jit(solution)/shard_map/stack | solution.py:319
  2.7 1.3 %copy.15 = bf16[8,2,16384]{2,1,0:T(2,128)(2,1)} copy(bf16[8,2,16384]{2,0,1:T(8,128)(2,1)S(1)} %pad_maximum_fusion) | data formatting | bytes 1048576 | tf_op jit(solution)/shard_map/stack | solution.py:319
  4.1 0.0 copy-start.9
  4.1 7.4 %all-to-all-start = ((bf16[8,2,16384]{2,1,0:T(2,128)(2,1)}), bf16[8,2,16384]{2,1,0:T(2,128)(2,1)S(1)}, u32[]{:S(2)}, u32[]{:S(2)}) async-start(bf16[8,2,16384]{2,1,0:T(2,128)(2,1)} %copy.15), calls=%async_computation | async-start | bytes 1048576 | tf_op jit(solution)/shard_map/all_to_all | solution.py:320
  11.5 0.0 copy-done.8
  11.5 38.6 %all_gather.3 = bf16[1,2,131072]{2,1,0:T(2,128)(2,1)S(1)} all-gather(bf16[1,2,16384]{2,1,0:T(2,128)(2,1)S(1)} %copy-done.8), channel_id=1, replica_groups=mesh['groups'=2,'segment'=8,'template'=2] {'segment'}, dimensions={2}, use_global_device_ids=true | all-gather | bytes 589824 | tf_op jit(solution)/shard_map/all_gather | solution.py:324
  50.0 0.2 copy.27
  50.3 0.0 copy-done.9
  50.3 0.2 dynamic-slice_reduce_fusion.1
  50.5 0.0 all-to-all-done
  50.5 1.5 %fusion.2 = (bf16[8,1,16384]{2,1,0:T(2,128)(2,1)}, bf16[8,1,16384]{2,1,0:T(2,128)(2,1)S(1)}) fusion(bf16[8,2,16384]{2,1,0:T(2,128)(2,1)S(1)} %all-to-all-done), kind=kLoop, calls=%fused_computation.14 | loop fusion | bytes 1048576 | tf_op jit(solution)/shard_map/slice | solution.py:321
  52.0 0.0 copy-start
  52.0 0.0 copy-start.1
  52.0 0.0 copy-start.2
  52.0 0.0 copy-start.4
  52.0 0.0 copy-start.5
  52.0 0.0 copy-start.7
  52.1 0.4 convolution_convert_fusion
  52.4 0.8 %concatenate.13 = bf16[128,1024]{1,0:T(8,128)(2,1)} reshape(bf16[8,16384]{1,0:T(8,128)(2,1)S(1)} %convolution_convert_fusion) | data formatting | bytes 524288 | tf_op jit(solution)/shard_map/concatenate | solution.py:323
  53.3 1.4 %convolution_convert_fusion.1 = bf16[8,16384]{1,0:T(8,128)(2,1)S(1)} fusion(bf16[8,1,16384]{2,1,0:T(2,128)(2,1)} %get-tuple-element.11, s32[8]{0:T(128)S(1)} %get-tuple-element.9), kind=kOutput, calls=%fused_computation.1 | convolution fusion | flops 2228288 | bytes 524320 | tf_op jit(solution)/shard_map/dot_general | solution.py:314
  54.7 0.8 %concatenate.12 = bf16[128,1024]{1,0:T(8,128)(2,1)} reshape(bf16[8,16384]{1,0:T(8,128)(2,1)S(1)} %convolution_convert_fusion.1) | data formatting | bytes 524288 | tf_op jit(solution)/shard_map/concatenate | solution.py:323
  55.5 1.1 %pad_maximum_fusion.1.segment_ref = bf16[256,1024]{1,0:T(8,128)(2,1)S(1)} fusion(bf16[128,1024]{1,0:T(8,128)(2,1)} %concatenate.13, bf16[128,1024]{1,0:T(8,128)(2,1)} %concatenate.12), kind=kLoop, calls=%fused_computation.4 | loop fusion | flops 1048576 | bytes 1048576 | tf_op jit(solution)/shard_map/concatenate | solution.py:323
  56.6 0.0 copy-done
  56.6 0.0 copy-done.1
  56.6 0.0 copy-done.2
  56.6 0.0 copy-done.4
  56.6 0.0 copy-done.5
  56.6 0.0 copy-done.7
  56.7 0.0 copy-start.6
  56.7 0.8 %copy-done.6 = bf16[128,256]{1,0:T(8,128)(2,1)S(1)} copy-done((bf16[128,256]{1,0:T(8,128)(2,1)S(1)}, bf16[128,256]{1,0:T(8,128)(2,1)}, u32[]{:S(2)}) %copy-start.6) | copy-done | bytes 65560
  57.5 14.3 %shard_map.121 = (bf16[64,2048]{1,0:T(8,128)(2,1)S(1)}, bf16[64,2048]{1,0:T(8,128)(2,1)S(1)}, f32[1,1]{1,0:T(1,128)}) custom-call(s32[1,3]{1,0:T(1,128)S(1)} %copy-done.7, bf16[256,1024]{1,0:T(8,128)(2,1)S(1)} %pad_maximum_fusion.1.segment_ref, bf16[128,2048]{1,0:T(8,128)(2,1)S(1)} %bitcast.18, bf16[512,256]{1,0:T(8,128)(2,1)S(1)} %copy-done.1, ...), custom_call_target="tpu_custom_call" | custom-call | tf_op jit(solution)/shard_map/pallas_call | solution.py:283
  71.8 0.0 copy-start.3
  71.8 0.7 copy-done.3
  72.5 2.1 %reshape.29 = bf16[1,1,131072]{2,1,0:T(2,128)(2,1)} reshape(bf16[64,2048]{1,0:T(8,128)(2,1)} %copy-done.3) | data formatting | bytes 524288 | tf_op jit(solution)/shard_map/reshape | solution.py:332
  74.7 1.1 %reshape.30 = bf16[1,1,131072]{2,1,0:T(2,128)(2,1)} reshape(bf16[64,2048]{1,0:T(8,128)(2,1)S(1)} %get-tuple-element.7) | data formatting | bytes 524288 | tf_op jit(solution)/shard_map/reshape | solution.py:332
  (2 shorter events, 0.1 us)
Async XLA Ops:
  0.6 10.8 %copy-start.8 = (bf16[1,2,16384]{2,1,0:T(2,128)(2,1)S(1)}, bf16[1,2,16384]{2,1,0:T(2,128)(2,1)}, u32[]{:S(2)}) copy-start(bf16[1,2,16384]{2,1,0:T(2,128)(2,1)} %param.12) | copy-start | bytes 196612
  4.1 46.2 %copy-start.9 = (s32[8,8]{1,0:T(8,128)S(1)}, s32[8,8]{1,0:T(8,128)}, u32[]{:S(2)}) copy-start(s32[8,8]{1,0:T(8,128)} %param.11) | copy-start | bytes 772
  4.1 46.4 %all-to-all-start = ((bf16[8,2,16384]{2,1,0:T(2,128)(2,1)}), bf16[8,2,16384]{2,1,0:T(2,128)(2,1)S(1)}, u32[]{:S(2)}, u32[]{:S(2)}) async-start(bf16[8,2,16384]{2,1,0:T(2,128)(2,1)} %copy.15), calls=%async_computation | async-start | bytes 1048576 | tf_op jit(solution)/shard_map/all_to_all | solution.py:320
  52.0 4.6 %copy-start = (f32[2,32,64,128]{3,2,1,0:T(8,128)S(1)}, f32[2,32,64,128]{3,2,1,0:T(8,128)}, u32[]{:S(2)}) copy-start(f32[2,32,64,128]{3,2,1,0:T(8,128)} %constant.32.clone.turn_one_ref) | copy-start | bytes 6291460
  52.0 4.6 %copy-start.1 = (bf16[512,256]{1,0:T(8,128)(2,1)S(1)}, bf16[512,256]{1,0:T(8,128)(2,1)}, u32[]{:S(2)}) copy-start(bf16[512,256]{1,0:T(8,128)(2,1)} %constant.28.clone.first_fwd_ref) | copy-start | bytes 786436
  52.0 4.6 %copy-start.2 = (f32[2,32,8,128]{3,2,1,0:T(8,128)S(1)}, f32[2,32,8,128]{3,2,1,0:T(8,128)}, u32[]{:S(2)}) copy-start(f32[2,32,8,128]{3,2,1,0:T(8,128)} %constant.33.clone.turn_two_ref) | copy-start | bytes 786436
  52.0 4.6 %copy-start.4 = (bf16[256,128]{1,0:T(8,128)(2,1)S(1)}, bf16[256,128]{1,0:T(8,128)(2,1)}, u32[]{:S(2)}) copy-start(bf16[256,128]{1,0:T(8,128)(2,1)} %constant.29.clone.first_inv_ref) | copy-start | bytes 196612
  52.0 4.6 %copy-start.5 = (bf16[128,256]{1,0:T(8,128)(2,1)S(1)}, bf16[128,256]{1,0:T(8,128)(2,1)}, u32[]{:S(2)}) copy-start(bf16[128,256]{1,0:T(8,128)(2,1)} %constant.30.clone.third_fwd_ref) | copy-start | bytes 196612
  52.0 4.6 %copy-start.7 = (s32[1,3]{1,0:T(1,128)S(1)}, s32[1,3]{1,0:T(1,128)}, u32[]{:S(2)}) copy-start(s32[1,3]{1,0:T(1,128)} %edges_ref.1) | copy-start | bytes 40
  56.7 0.8 %copy-start.6 = (bf16[128,256]{1,0:T(8,128)(2,1)S(1)}, bf16[128,256]{1,0:T(8,128)(2,1)}, u32[]{:S(2)}) copy-start(bf16[128,256]{1,0:T(8,128)(2,1)} %constant.31.clone.third_inv_ref) | copy-start | bytes 196612
  71.8 0.7 copy-start.3

commit v2 on v1

--- a/solution.py
+++ b/solution.py
@@ -1,3 +1,4 @@
+import functools
 import functools
 import math
 
@@ -153,7 +154,8 @@
 
 def compute_kernel(
     edges_ref,
-    segment_ref,
+    slot_ref,
+    received_ref,
     template_ref,
     first_fwd_ref,
     first_inv_ref,
@@ -169,7 +171,19 @@
     turned_ref,
     corr_ref,
     piece_ref,
+    segment_ref,
+    in_order,
 ):
+    if in_order:
+        segment_ref = received_ref
+    else:
+        position = lax.axis_index("segment")
+        for kind in range(2):
+            half = jnp.minimum(position + kind, 7)
+            for source in range(8):
+                place = pl.multiple_of((kind * 8 + slot_ref[source, half]) * 16, 16)
+                begin = (kind * 8 + source) * 16
+                segment_ref[pl.ds(place, 16), :] = received_ref[begin : begin + 16, :]
     level_fwd_ref[...] = jnp.dot(
         first_fwd_ref[...], segment_ref[...], preferred_element_type=F32
     )
@@ -278,16 +292,17 @@
     peak_ref[...] = jnp.max(best, axis=(0, 1), keepdims=True)
 
 
-def compute(edges, segment, template):
+def compute(edges, slots, segment, template, in_order):
     vmem = pl.BlockSpec(memory_space=pltpu.VMEM)
+    smem = pl.BlockSpec(memory_space=pltpu.SMEM)
     return pl.pallas_call(
-        compute_kernel,
+        functools.partial(compute_kernel, in_order=in_order),
         out_shape=(
             jax.ShapeDtypeStruct((RADIX_A, WIDE), BF16),
             jax.ShapeDtypeStruct((RADIX_A, WIDE), BF16),
             jax.ShapeDtypeStruct((1, 1), F32),
         ),
-        in_specs=[pl.BlockSpec(memory_space=pltpu.SMEM)] + [vmem] * 8,
+        in_specs=[smem] * 2 + [vmem] * 8,
         out_specs=(vmem, vmem, vmem),
         scratch_shapes=[
             pltpu.VMEM((SUBROWS * 2 * RADIX_A, INNER // SUBROWS), F32),
@@ -295,9 +310,10 @@
             pltpu.VMEM((WIDE, 2 * RADIX_C), F32),
             pltpu.VMEM((2 * RADIX_A, WIDE), F32),
             pltpu.VMEM((4, 2 * RADIX_A, WIDE), F32),
+            pltpu.VMEM((RADIX_A * SUBROWS, INNER // SUBROWS), BF16),
         ],
         compiler_params=pltpu.CompilerParams(vmem_limit_bytes=40 * 1024 * 1024),
-    )(edges, segment, template, *[jnp.asarray(t) for t in tables()])
+    )(edges, slots, segment, template, *[jnp.asarray(t) for t in tables()])
 
 
 def move_general(strain_frames, frame_slot, templates):
@@ -326,9 +342,116 @@
     return segment, template
 
 
+def move_kernel(frames_ref, block_ref, frames_out, blocks_out, local_sem, send, recv):
+    me = lax.axis_index("segment")
+    core = lax.axis_index("template")
+    other = {"template": 1 - core}
+    beside = {"segment": me + 1 - 2 * (me % 2)}
+
+    def after(step):
+        return (me + step) % 8
+
+    barrier = pltpu.get_barrier_semaphore()
+    for step in range(1, 8):
+        pl.semaphore_signal(
+            barrier, inc=1, device_id={"segment": after(step)}, device_id_type=pl.DeviceIdType.MESH
+        )
+    pl.semaphore_signal(barrier, inc=1, device_id=other, device_id_type=pl.DeviceIdType.MESH)
+    pl.semaphore_wait(barrier, 8)
+
+    def remote(source, target, row, step, device):
+        return pltpu.make_async_remote_copy(
+            src_ref=source,
+            dst_ref=target,
+            send_sem=send.at[row, step],
+            recv_sem=recv.at[row, step],
+            device_id=device,
+            device_id_type=pl.DeviceIdType.MESH,
+        )
+
+    own_frame = frames_ref.at[me + core]
+    local_frame = pltpu.make_async_copy(own_frame, frames_out.at[core, me], local_sem.at[0])
+    local_block = pltpu.make_async_copy(block_ref, blocks_out.at[me], local_sem.at[1])
+    sends = []
+
+    def begin(copy):
+        copy.start()
+        sends.append(copy)
+
+    for step in FAR_FIRST:
+        there = after(step)
+        begin(
+            remote(
+                frames_ref.at[there + core],
+                frames_out.at[core, me],
+                0,
+                step,
+                {"segment": there},
+            )
+        )
+        if step % 2 == 0:
+            begin(remote(block_ref, blocks_out.at[me], 2, step, {"segment": there}))
+    begin(remote(own_frame, frames_out.at[core, me], 1, 0, other))
+    begin(remote(block_ref, blocks_out.at[me], 3, 0, beside))
+    local_frame.start()
+    local_block.start()
+    for step in NEAR_FIRST:
+        source = after(8 - step)
+        slot = frames_out.at[core, source]
+        remote(slot, slot, 0, step, {"segment": source}).wait_recv()
+        begin(remote(slot, slot, 1, step, other))
+        if step % 2 == 0:
+            slot = blocks_out.at[source]
+            remote(slot, slot, 2, step, {"segment": source}).wait_recv()
+            begin(remote(slot, slot, 3, step, beside))
+    local_frame.wait()
+    local_block.wait()
+    neighbour = me + 1 - 2 * (me % 2)
+    for step in range(8):
+        slot = frames_out.at[1 - core, after(8 - step)]
+        remote(slot, slot, 1, step, other).wait_recv()
+        if step % 2 == 0:
+            slot = blocks_out.at[(neighbour + 8 - step) % 8]
+            remote(slot, slot, 3, step, beside).wait_recv()
+    for copy in sends:
+        copy.wait_send()
+
+
+FAR_FIRST = (4, 6, 2, 5, 3, 7, 1)
+NEAR_FIRST = (1, 7, 2, 6, 3, 5, 4)
+
+
+def move(strain_frames, templates):
+    frames = jnp.concatenate(
+        [strain_frames.reshape(8, 16, 1024), jnp.zeros((1, 16, 1024), BF16)], axis=0
+    )
+    block = templates.reshape(16, WIDE)
+    anywhere = pl.BlockSpec(memory_space=pl.ANY)
+    received, blocks = pl.pallas_call(
+        move_kernel,
+        out_shape=(
+            jax.ShapeDtypeStruct((2, 8, 16, 1024), BF16),
+            jax.ShapeDtypeStruct((8, 16, WIDE), BF16),
+        ),
+        in_specs=[anywhere, anywhere],
+        out_specs=(anywhere, anywhere),
+        scratch_shapes=[
+            pltpu.SemaphoreType.DMA((2,)),
+            pltpu.SemaphoreType.DMA((4, 8)),
+            pltpu.SemaphoreType.DMA((4, 8)),
+        ],
+        compiler_params=pltpu.CompilerParams(collective_id=0, has_side_effects=True),
+    )(frames, block)
+    return received.reshape(256, 1024), blocks.reshape(2 * RADIX_A, WIDE)
+
+
 def local(strain_frames, frame_slot, templates, bin_edges):
-    segment, template = move_general(strain_frames, frame_slot, templates)
-    snr, chisq, peak = compute(bin_edges, segment, template)
+    direct = lax.axis_size("segment") == 8 and strain_frames.shape[1] == 16384
+    if direct:
+        segment, template = move(strain_frames, templates)
+    else:
+        segment, template = move_general(strain_frames, frame_slot, templates)
+    snr, chisq, peak = compute(bin_edges, frame_slot, segment, template, not direct)
     return (snr.reshape(1, 1, KEPT), chisq.reshape(1, 1, KEPT), peak)
 
 

time: 76.2 us -> 54.4 us (0.71)
  the two profiles are of different devices: /device:TPU:0 before, /device:TPU:8 now
where the time goes in v2:
time: 54.4 us; the launch traced here: 53.8 us
  Pallas kernels  38.1 us (70%)
  local copies, waits for them, and re-layouts  15 us (28%)
  between operations  0.66 us (1%)
    pallas_call x1, Pallas kernels, move(): pl.pallas_call(move_kernel, out_shape=(jax.ShapeDtypeStruct((2, 8, 16, 10...  23.6 us
    pallas_call x1, Pallas kernels, compute(): pl.pallas_call(functools.partial(compute_kernel, in_order=in_order), out_...  14.6 us
    unnamed x21, local copies, waits for them, and re-layouts  10.5 us
    reshape x2, local copies, waits for them, and re-layouts, local(): return (snr.reshape(1, 1, KEPT), chisq.reshape(1, 1, KEPT), peak)  2.27 us
    reshape x1, local copies, waits for them, and re-layouts, move(): block = templates.reshape(16, WIDE)  1.5 us

profile of v2, /device:TPU:8, one launch (start us, length us, event | category | flops | bytes accessed | tf_op | source)
XLA Modules:
  0.0 53.8 jit_solution(2455600086246733934)
XLA Ops:
  0.6 1.5 %reshape.25.block_ref = bf16[16,2048]{1,0:T(8,128)(2,1)} reshape(bf16[1,2,16384]{2,1,0:T(2,128)(2,1)} %param.12) | data formatting | bytes 131072 | tf_op jit(solution)/shard_map/reshape | solution.py:428
  2.1 1.1 %copy.15 = bf16[1,8,16,1024]{3,2,1,0:T(8,128)(2,1)S(1)} copy(bf16[1,8,16,1024]{3,1,2,0:T(8,128)(2,1)} %bitcast.9) | data formatting | bytes 524288
  3.2 0.7 %concatenate.3.frames_ref = bf16[9,16,1024]{2,1,0:T(8,128)(2,1)} pad(bf16[8,16,1024]{2,1,0:T(8,128)(2,1)S(1)} %bitcast.8, bf16[]{:T(256)} %constant.6.clone.1), padding=0_1x0_0x0_0 | pad | bytes 557058 | tf_op jit(solution)/shard_map/concatenate | solution.py:425
  4.0 23.6 %shard_map.121 = (bf16[2,8,16,1024]{3,2,1,0:T(8,128)(2,1)}, bf16[8,16,2048]{2,1,0:T(8,128)(2,1)}) custom-call(bf16[9,16,1024]{2,1,0:T(8,128)(2,1)} %concatenate.3.frames_ref, bf16[16,2048]{1,0:T(8,128)(2,1)} %reshape.25.block_ref), custom_call_target="tpu_custom_call" | custom-call | tf_op jit(solution)/shard_map/pallas_call | solution.py:430
  27.5 0.0 copy-start
  27.6 1.6 %copy-done = f32[2,32,64,128]{3,2,1,0:T(8,128)S(1)} copy-done((f32[2,32,64,128]{3,2,1,0:T(8,128)S(1)}, f32[2,32,64,128]{3,2,1,0:T(8,128)}, u32[]{:S(2)}) %copy-start) | copy-done | bytes 2097176
  29.1 0.0 copy-start.1
  29.1 1.0 %copy-done.1 = bf16[2,8,16,1024]{3,2,1,0:T(8,128)(2,1)S(1)} copy-done((bf16[2,8,16,1024]{3,2,1,0:T(8,128)(2,1)S(1)}, bf16[2,8,16,1024]{3,2,1,0:T(8,128)(2,1)}, u32[]{:S(2)}) %copy-start.1) | copy-done | bytes 524312
  30.2 0.0 copy-start.2
  30.2 1.0 %copy-done.2 = bf16[8,16,2048]{2,1,0:T(8,128)(2,1)S(1)} copy-done((bf16[8,16,2048]{2,1,0:T(8,128)(2,1)S(1)}, bf16[8,16,2048]{2,1,0:T(8,128)(2,1)}, u32[]{:S(2)}) %copy-start.2) | copy-done | bytes 524312
  31.2 0.0 copy-start.3
  31.2 0.9 %copy-done.3 = f32[2,32,8,128]{3,2,1,0:T(8,128)S(1)} copy-done((f32[2,32,8,128]{3,2,1,0:T(8,128)S(1)}, f32[2,32,8,128]{3,2,1,0:T(8,128)}, u32[]{:S(2)}) %copy-start.3) | copy-done | bytes 262168
  32.2 0.0 copy-start.4
  32.2 0.9 %copy-done.4 = bf16[512,256]{1,0:T(8,128)(2,1)S(1)} copy-done((bf16[512,256]{1,0:T(8,128)(2,1)S(1)}, bf16[512,256]{1,0:T(8,128)(2,1)}, u32[]{:S(2)}) %copy-start.4) | copy-done | bytes 262168
  33.1 0.0 copy-start.5
  33.1 0.8 %copy-done.5 = bf16[128,256]{1,0:T(8,128)(2,1)S(1)} copy-done((bf16[128,256]{1,0:T(8,128)(2,1)S(1)}, bf16[128,256]{1,0:T(8,128)(2,1)}, u32[]{:S(2)}) %copy-start.5) | copy-done | bytes 65560
  34.0 0.0 copy-start.6
  34.0 0.8 %copy-done.6 = bf16[128,256]{1,0:T(8,128)(2,1)S(1)} copy-done((bf16[128,256]{1,0:T(8,128)(2,1)S(1)}, bf16[128,256]{1,0:T(8,128)(2,1)}, u32[]{:S(2)}) %copy-start.6) | copy-done | bytes 65560
  34.8 0.0 copy-start.7
  34.8 0.8 %copy-done.7 = bf16[256,128]{1,0:T(8,128)(2,1)S(1)} copy-done((bf16[256,128]{1,0:T(8,128)(2,1)S(1)}, bf16[256,128]{1,0:T(8,128)(2,1)}, u32[]{:S(2)}) %copy-start.7) | copy-done | bytes 65560
  35.6 0.0 copy-start.8
  35.6 0.7 %copy-done.8 = s32[8,8]{1,0:T(8,128)S(1)} copy-done((s32[8,8]{1,0:T(8,128)S(1)}, s32[8,8]{1,0:T(8,128)}, u32[]{:S(2)}) %copy-start.8) | copy-done | bytes 280
  36.3 0.0 copy-start.9
  36.3 0.7 %copy-done.9 = s32[1,3]{1,0:T(1,128)S(1)} copy-done((s32[1,3]{1,0:T(1,128)S(1)}, s32[1,3]{1,0:T(1,128)}, u32[]{:S(2)}) %copy-start.9) | copy-done | bytes 36
  37.0 14.6 %shard_map.122 = (bf16[64,2048]{1,0:T(8,128)(2,1)S(1)}, bf16[64,2048]{1,0:T(8,128)(2,1)S(1)}, f32[1,1]{1,0:T(1,128)}) custom-call(s32[1,3]{1,0:T(1,128)S(1)} %copy-done.9, s32[8,8]{1,0:T(8,128)S(1)} %copy-done.8, bf16[256,1024]{1,0:T(8,128)(2,1)S(1)} %bitcast.6, bf16[128,2048]{1,0:T(8,128)(2,1)S(1)} %bitcast.7, bf16[512,256]{1,0:T(8,128)(2,1)S(1)} %copy-done.4, ...), custom_call_target="tpu_custom_call" | custom-call | tf_op jit(solution)/shard_map/pallas_call | solution.py:298
  51.5 1.1 %reshape.28 = bf16[1,1,131072]{2,1,0:T(2,128)(2,1)} reshape(bf16[64,2048]{1,0:T(8,128)(2,1)S(1)} %get-tuple-element.10) | data formatting | bytes 524288 | tf_op jit(solution)/shard_map/reshape | solution.py:455
  52.7 1.1 %reshape.29 = bf16[1,1,131072]{2,1,0:T(2,128)(2,1)} reshape(bf16[64,2048]{1,0:T(8,128)(2,1)S(1)} %get-tuple-element.11) | data formatting | bytes 524288 | tf_op jit(solution)/shard_map/reshape | solution.py:455
Async XLA Ops:
  27.5 1.6 %copy-start = (f32[2,32,64,128]{3,2,1,0:T(8,128)S(1)}, f32[2,32,64,128]{3,2,1,0:T(8,128)}, u32[]{:S(2)}) copy-start(f32[2,32,64,128]{3,2,1,0:T(8,128)} %constant.18.clone.turn_one_ref) | copy-start | bytes 6291460
  29.1 1.0 %copy-start.1 = (bf16[2,8,16,1024]{3,2,1,0:T(8,128)(2,1)S(1)}, bf16[2,8,16,1024]{3,2,1,0:T(8,128)(2,1)}, u32[]{:S(2)}) copy-start(bf16[2,8,16,1024]{3,2,1,0:T(8,128)(2,1)} %get-tuple-element.8) | copy-start | bytes 1572868
  30.2 1.0 %copy-start.2 = (bf16[8,16,2048]{2,1,0:T(8,128)(2,1)S(1)}, bf16[8,16,2048]{2,1,0:T(8,128)(2,1)}, u32[]{:S(2)}) copy-start(bf16[8,16,2048]{2,1,0:T(8,128)(2,1)} %get-tuple-element.9) | copy-start | bytes 1572868
  31.2 0.9 %copy-start.3 = (f32[2,32,8,128]{3,2,1,0:T(8,128)S(1)}, f32[2,32,8,128]{3,2,1,0:T(8,128)}, u32[]{:S(2)}) copy-start(f32[2,32,8,128]{3,2,1,0:T(8,128)} %constant.19.clone.turn_two_ref) | copy-start | bytes 786436
  32.2 0.9 %copy-start.4 = (bf16[512,256]{1,0:T(8,128)(2,1)S(1)}, bf16[512,256]{1,0:T(8,128)(2,1)}, u32[]{:S(2)}) copy-start(bf16[512,256]{1,0:T(8,128)(2,1)} %constant.14.clone.first_fwd_ref) | copy-start | bytes 786436
  33.1 0.8 %copy-start.5 = (bf16[128,256]{1,0:T(8,128)(2,1)S(1)}, bf16[128,256]{1,0:T(8,128)(2,1)}, u32[]{:S(2)}) copy-start(bf16[128,256]{1,0:T(8,128)(2,1)} %constant.17.clone.third_inv_ref) | copy-start | bytes 196612
  34.0 0.8 %copy-start.6 = (bf16[128,256]{1,0:T(8,128)(2,1)S(1)}, bf16[128,256]{1,0:T(8,128)(2,1)}, u32[]{:S(2)}) copy-start(bf16[128,256]{1,0:T(8,128)(2,1)} %constant.16.clone.third_fwd_ref) | copy-start | bytes 196612
  34.8 0.8 %copy-start.7 = (bf16[256,128]{1,0:T(8,128)(2,1)S(1)}, bf16[256,128]{1,0:T(8,128)(2,1)}, u32[]{:S(2)}) copy-start(bf16[256,128]{1,0:T(8,128)(2,1)} %constant.15.clone.first_inv_ref) | copy-start | bytes 196612
  35.6 0.7 %copy-start.8 = (s32[8,8]{1,0:T(8,128)S(1)}, s32[8,8]{1,0:T(8,128)}, u32[]{:S(2)}) copy-start(s32[8,8]{1,0:T(8,128)} %slot_ref.1) | copy-start | bytes 772
  36.3 0.7 %copy-start.9 = (s32[1,3]{1,0:T(1,128)S(1)}, s32[1,3]{1,0:T(1,128)}, u32[]{:S(2)}) copy-start(s32[1,3]{1,0:T(1,128)} %edges_ref.1) | copy-start | bytes 40

commit v3 on v2

--- a/solution.py
+++ b/solution.py
@@ -152,28 +152,20 @@
         )
 
 
-def compute_kernel(
-    edges_ref,
-    slot_ref,
-    received_ref,
-    template_ref,
-    first_fwd_ref,
-    first_inv_ref,
-    third_fwd_ref,
-    third_inv_ref,
-    turn_one_ref,
-    turn_two_ref,
-    snr_ref,
-    chisq_ref,
-    peak_ref,
-    level_fwd_ref,
-    level_inv_ref,
-    turned_ref,
-    corr_ref,
-    piece_ref,
-    segment_ref,
-    in_order,
-):
+def compute_kernel(edges_ref, slot_ref, *refs, in_order):
+    sources, refs = refs[:8], refs[8:]
+    snr_ref, chisq_ref, peak_ref = refs[:3]
+    level_fwd_ref, level_inv_ref, turned_ref, corr_ref, piece_ref, segment_ref = refs[3:9]
+    places, fetch_sem = refs[9:17], refs[17]
+    fetches = [
+        pltpu.make_async_copy(source, place, fetch_sem.at[number])
+        for number, (source, place) in enumerate(zip(sources, places))
+    ]
+    for number in (0, 2, 6, 7, 4, 1, 3, 5):
+        fetches[number].start()
+    received_ref, template_ref, first_fwd_ref, first_inv_ref = places[:4]
+    third_fwd_ref, third_inv_ref, turn_one_ref, turn_two_ref = places[4:]
+    fetches[0].wait()
     if in_order:
         segment_ref = received_ref
     else:
@@ -184,15 +176,21 @@
                 place = pl.multiple_of((kind * 8 + slot_ref[source, half]) * 16, 16)
                 begin = (kind * 8 + source) * 16
                 segment_ref[pl.ds(place, 16), :] = received_ref[begin : begin + 16, :]
+    fetches[2].wait()
     level_fwd_ref[...] = jnp.dot(
         first_fwd_ref[...], segment_ref[...], preferred_element_type=F32
     )
+    fetches[6].wait()
+    fetches[7].wait()
     middle(level_fwd_ref, 8, -1, turn_one_ref, turn_two_ref, turned_ref)
 
     def keep_spectrum(lanes, value):
         corr_ref[:, lanes] = value
 
+    fetches[4].wait()
     last(third_fwd_ref, turned_ref, keep_spectrum)
+    for number in (1, 3, 5):
+        fetches[number].wait()
     edges = [edges_ref[0, e] for e in range(3)]
     column = lax.broadcasted_iota(jnp.int32, (8, WIDE), 1)
     row = lax.broadcasted_iota(jnp.int32, (8, WIDE), 0)
@@ -295,6 +293,7 @@
 def compute(edges, slots, segment, template, in_order):
     vmem = pl.BlockSpec(memory_space=pltpu.VMEM)
     smem = pl.BlockSpec(memory_space=pltpu.SMEM)
+    operands = [segment, template] + [jnp.asarray(t) for t in tables()]
     return pl.pallas_call(
         functools.partial(compute_kernel, in_order=in_order),
         out_shape=(
@@ -302,7 +301,7 @@
             jax.ShapeDtypeStruct((RADIX_A, WIDE), BF16),
             jax.ShapeDtypeStruct((1, 1), F32),
         ),
-        in_specs=[smem] * 2 + [vmem] * 8,
+        in_specs=[smem] * 2 + [pl.BlockSpec(memory_space=pltpu.HBM)] * 8,
         out_specs=(vmem, vmem, vmem),
         scratch_shapes=[
             pltpu.VMEM((SUBROWS * 2 * RADIX_A, INNER // SUBROWS), F32),
@@ -311,9 +310,11 @@
             pltpu.VMEM((2 * RADIX_A, WIDE), F32),
             pltpu.VMEM((4, 2 * RADIX_A, WIDE), F32),
             pltpu.VMEM((RADIX_A * SUBROWS, INNER // SUBROWS), BF16),
-        ],
+        ]
+        + [pltpu.VMEM(operand.shape, operand.dtype) for operand in operands]
+        + [pltpu.SemaphoreType.DMA((8,))],
         compiler_params=pltpu.CompilerParams(vmem_limit_bytes=40 * 1024 * 1024),
-    )(edges, slots, segment, template, *[jnp.asarray(t) for t in tables()])
+    )(edges, slots, *operands)
 
 
 def move_general(strain_frames, frame_slot, templates):
@@ -342,11 +343,21 @@
     return segment, template
 
 
-def move_kernel(frames_ref, block_ref, frames_out, blocks_out, local_sem, send, recv):
+def move_kernel(
+    strain_ref,
+    template_ref,
+    frames_out,
+    blocks_out,
+    wide_ref,
+    frames_ref,
+    block_ref,
+    local_sem,
+    send,
+    recv,
+):
     me = lax.axis_index("segment")
     core = lax.axis_index("template")
     other = {"template": 1 - core}
-    beside = {"segment": me + 1 - 2 * (me % 2)}
 
     def after(step):
         return (me + step) % 8
@@ -357,6 +368,14 @@
             barrier, inc=1, device_id={"segment": after(step)}, device_id_type=pl.DeviceIdType.MESH
         )
     pl.semaphore_signal(barrier, inc=1, device_id=other, device_id_type=pl.DeviceIdType.MESH)
+    parts = [template_ref[0, :, row * WIDE : (row + 1) * WIDE].astype(F32) for row in range(8)]
+    rows = [p[c : c + 1] for c in range(2) for p in parts]
+    block_ref[...] = jnp.concatenate(rows, axis=0).astype(BF16)
+    for row in range(16):
+        wide_ref[:, row, :] = strain_ref[:, row * 1024 : (row + 1) * 1024].astype(F32)
+    for frame in range(8):
+        frames_ref[frame] = wide_ref[frame].astype(BF16)
+    frames_ref[8] = jnp.zeros((16, 1024), BF16)
     pl.semaphore_wait(barrier, 8)
 
     def remote(source, target, row, step, device):
@@ -389,10 +408,9 @@
                 {"segment": there},
             )
         )
-        if step % 2 == 0:
-            begin(remote(block_ref, blocks_out.at[me], 2, step, {"segment": there}))
+    for step in FAR_FIRST:
+        begin(remote(block_ref, blocks_out.at[me], 2, step, {"segment": after(step)}))
     begin(remote(own_frame, frames_out.at[core, me], 1, 0, other))
-    begin(remote(block_ref, blocks_out.at[me], 3, 0, beside))
     local_frame.start()
     local_block.start()
     for step in NEAR_FIRST:
@@ -400,19 +418,15 @@
         slot = frames_out.at[core, source]
         remote(slot, slot, 0, step, {"segment": source}).wait_recv()
         begin(remote(slot, slot, 1, step, other))
-        if step % 2 == 0:
+    local_frame.wait()
+    local_block.wait()
+    for step in range(8):
+        source = after(8 - step)
+        slot = frames_out.at[1 - core, source]
+        remote(slot, slot, 1, step, other).wait_recv()
+        if step:
             slot = blocks_out.at[source]
             remote(slot, slot, 2, step, {"segment": source}).wait_recv()
-            begin(remote(slot, slot, 3, step, beside))
-    local_frame.wait()
-    local_block.wait()
-    neighbour = me + 1 - 2 * (me % 2)
-    for step in range(8):
-        slot = frames_out.at[1 - core, after(8 - step)]
-        remote(slot, slot, 1, step, other).wait_recv()
-        if step % 2 == 0:
-            slot = blocks_out.at[(neighbour + 8 - step) % 8]
-            remote(slot, slot, 3, step, beside).wait_recv()
     for copy in sends:
         copy.wait_send()
 
@@ -422,26 +436,26 @@
 
 
 def move(strain_frames, templates):
-    frames = jnp.concatenate(
-        [strain_frames.reshape(8, 16, 1024), jnp.zeros((1, 16, 1024), BF16)], axis=0
-    )
-    block = templates.reshape(16, WIDE)
     anywhere = pl.BlockSpec(memory_space=pl.ANY)
+    vmem = pl.BlockSpec(memory_space=pltpu.VMEM)
     received, blocks = pl.pallas_call(
         move_kernel,
         out_shape=(
             jax.ShapeDtypeStruct((2, 8, 16, 1024), BF16),
             jax.ShapeDtypeStruct((8, 16, WIDE), BF16),
         ),
-        in_specs=[anywhere, anywhere],
+        in_specs=[vmem, vmem],
         out_specs=(anywhere, anywhere),
         scratch_shapes=[
+            pltpu.VMEM((8, 16, 1024), F32),
+            pltpu.VMEM((9, 16, 1024), BF16),
+            pltpu.VMEM((16, WIDE), BF16),
             pltpu.SemaphoreType.DMA((2,)),
-            pltpu.SemaphoreType.DMA((4, 8)),
-            pltpu.SemaphoreType.DMA((4, 8)),
+            pltpu.SemaphoreType.DMA((3, 8)),
+            pltpu.SemaphoreType.DMA((3, 8)),
         ],
         compiler_params=pltpu.CompilerParams(collective_id=0, has_side_effects=True),
-    )(frames, block)
+    )(strain_frames, templates)
     return received.reshape(256, 1024), blocks.reshape(2 * RADIX_A, WIDE)
 
 

time: 54.4 us -> 53.2 us (0.978)
  the two profiles are of different devices: /device:TPU:8 before, /device:TPU:0 now
where the time goes in v3:
time: 53.2 us; the launch traced here: 52.7 us
  Pallas kernels  40.4 us (76%)
  local copies, waits for them, and re-layouts  11.7 us (22%)
  between operations  0.66 us (1%)
    pallas_call x1, Pallas kernels, move(): pl.pallas_call(move_kernel, out_shape=(jax.ShapeDtypeStruct((2, 8, 16, 10...  25.4 us
    pallas_call x1, Pallas kernels, compute(): pl.pallas_call(functools.partial(compute_kernel, in_order=in_order), out_...  15 us
    unnamed x20, local copies, waits for them, and re-layouts  9.43 us
    reshape x2, local copies, waits for them, and re-layouts, local(): return (snr.reshape(1, 1, KEPT), chisq.reshape(1, 1, KEPT), peak)  2.27 us

profile of v3, /device:TPU:0, one launch (start us, length us, event | category | flops | bytes accessed | tf_op | source)
XLA Modules:
  0.0 52.7 jit_solution(7630075128242918099)
XLA Ops:
  0.6 25.4 %shard_map.121 = (bf16[2,8,16,1024]{3,2,1,0:T(8,128)(2,1)}, bf16[8,16,2048]{2,1,0:T(8,128)(2,1)}) custom-call(bf16[8,16384]{1,0:T(8,128)(2,1)} %strain_ref.1, bf16[1,2,16384]{2,1,0:T(2,128)(2,1)} %template_ref.1), custom_call_target="tpu_custom_call" | custom-call | tf_op jit(solution)/shard_map/pallas_call | solution.py:441
  26.0 0.0 copy-start
  26.0 1.6 %copy-done = f32[2,32,64,128]{3,2,1,0:T(8,128)S(1)} copy-done((f32[2,32,64,128]{3,2,1,0:T(8,128)S(1)}, f32[2,32,64,128]{3,2,1,0:T(8,128)}, u32[]{:S(2)}) %copy-start) | copy-done | bytes 2097176
  27.6 0.0 copy-start.1
  27.6 1.0 %copy-done.1 = bf16[2,8,16,1024]{3,2,1,0:T(8,128)(2,1)S(1)} copy-done((bf16[2,8,16,1024]{3,2,1,0:T(8,128)(2,1)S(1)}, bf16[2,8,16,1024]{3,2,1,0:T(8,128)(2,1)}, u32[]{:S(2)}) %copy-start.1) | copy-done | bytes 524312
  28.6 0.0 copy-start.2
  28.6 1.0 %copy-done.2 = bf16[8,16,2048]{2,1,0:T(8,128)(2,1)S(1)} copy-done((bf16[8,16,2048]{2,1,0:T(8,128)(2,1)S(1)}, bf16[8,16,2048]{2,1,0:T(8,128)(2,1)}, u32[]{:S(2)}) %copy-start.2) | copy-done | bytes 524312
  29.7 0.0 copy-start.3
  29.7 0.9 %copy-done.3 = f32[2,32,8,128]{3,2,1,0:T(8,128)S(1)} copy-done((f32[2,32,8,128]{3,2,1,0:T(8,128)S(1)}, f32[2,32,8,128]{3,2,1,0:T(8,128)}, u32[]{:S(2)}) %copy-start.3) | copy-done | bytes 262168
  30.6 0.0 copy-start.4
  30.6 0.9 %copy-done.4 = bf16[512,256]{1,0:T(8,128)(2,1)S(1)} copy-done((bf16[512,256]{1,0:T(8,128)(2,1)S(1)}, bf16[512,256]{1,0:T(8,128)(2,1)}, u32[]{:S(2)}) %copy-start.4) | copy-done | bytes 262168
  31.6 0.0 copy-start.5
  31.6 0.8 %copy-done.5 = bf16[128,256]{1,0:T(8,128)(2,1)S(1)} copy-done((bf16[128,256]{1,0:T(8,128)(2,1)S(1)}, bf16[128,256]{1,0:T(8,128)(2,1)}, u32[]{:S(2)}) %copy-start.5) | copy-done | bytes 65560
  32.4 0.0 copy-start.6
  32.4 0.8 %copy-done.6 = bf16[128,256]{1,0:T(8,128)(2,1)S(1)} copy-done((bf16[128,256]{1,0:T(8,128)(2,1)S(1)}, bf16[128,256]{1,0:T(8,128)(2,1)}, u32[]{:S(2)}) %copy-start.6) | copy-done | bytes 65560
  33.3 0.0 copy-start.7
  33.3 0.8 %copy-done.7 = bf16[256,128]{1,0:T(8,128)(2,1)S(1)} copy-done((bf16[256,128]{1,0:T(8,128)(2,1)S(1)}, bf16[256,128]{1,0:T(8,128)(2,1)}, u32[]{:S(2)}) %copy-start.7) | copy-done | bytes 65560
  34.1 0.0 copy-start.8
  34.1 0.7 %copy-done.8 = s32[8,8]{1,0:T(8,128)S(1)} copy-done((s32[8,8]{1,0:T(8,128)S(1)}, s32[8,8]{1,0:T(8,128)}, u32[]{:S(2)}) %copy-start.8) | copy-done | bytes 280
  34.8 0.0 copy-start.9
  34.8 0.7 %copy-done.9 = s32[1,3]{1,0:T(1,128)S(1)} copy-done((s32[1,3]{1,0:T(1,128)S(1)}, s32[1,3]{1,0:T(1,128)}, u32[]{:S(2)}) %copy-start.9) | copy-done | bytes 36
  35.4 15.0 %shard_map.122 = (bf16[64,2048]{1,0:T(8,128)(2,1)S(1)}, bf16[64,2048]{1,0:T(8,128)(2,1)S(1)}, f32[1,1]{1,0:T(1,128)}) custom-call(s32[1,3]{1,0:T(1,128)S(1)} %copy-done.9, s32[8,8]{1,0:T(8,128)S(1)} %copy-done.8, bf16[256,1024]{1,0:T(8,128)(2,1)S(1)} %bitcast.2, bf16[128,2048]{1,0:T(8,128)(2,1)S(1)} %bitcast.3, bf16[512,256]{1,0:T(8,128)(2,1)S(1)} %copy-done.4, ...), custom_call_target="tpu_custom_call" | custom-call | tf_op jit(solution)/shard_map/pallas_call | solution.py:297
  50.5 1.1 %reshape.20 = bf16[1,1,131072]{2,1,0:T(2,128)(2,1)} reshape(bf16[64,2048]{1,0:T(8,128)(2,1)S(1)} %get-tuple-element.10) | data formatting | bytes 524288 | tf_op jit(solution)/shard_map/reshape | solution.py:469
  51.6 1.1 %reshape.21 = bf16[1,1,131072]{2,1,0:T(2,128)(2,1)} reshape(bf16[64,2048]{1,0:T(8,128)(2,1)S(1)} %get-tuple-element.11) | data formatting | bytes 524288 | tf_op jit(solution)/shard_map/reshape | solution.py:469
Async XLA Ops:
  26.0 1.6 %copy-start = (f32[2,32,64,128]{3,2,1,0:T(8,128)S(1)}, f32[2,32,64,128]{3,2,1,0:T(8,128)}, u32[]{:S(2)}) copy-start(f32[2,32,64,128]{3,2,1,0:T(8,128)} %constant.16.clone.refs_6_) | copy-start | bytes 6291460
  27.6 1.0 %copy-start.1 = (bf16[2,8,16,1024]{3,2,1,0:T(8,128)(2,1)S(1)}, bf16[2,8,16,1024]{3,2,1,0:T(8,128)(2,1)}, u32[]{:S(2)}) copy-start(bf16[2,8,16,1024]{3,2,1,0:T(8,128)(2,1)} %get-tuple-element.8) | copy-start | bytes 1572868
  28.6 1.0 %copy-start.2 = (bf16[8,16,2048]{2,1,0:T(8,128)(2,1)S(1)}, bf16[8,16,2048]{2,1,0:T(8,128)(2,1)}, u32[]{:S(2)}) copy-start(bf16[8,16,2048]{2,1,0:T(8,128)(2,1)} %get-tuple-element.9) | copy-start | bytes 1572868
  29.7 0.9 %copy-start.3 = (f32[2,32,8,128]{3,2,1,0:T(8,128)S(1)}, f32[2,32,8,128]{3,2,1,0:T(8,128)}, u32[]{:S(2)}) copy-start(f32[2,32,8,128]{3,2,1,0:T(8,128)} %constant.17.clone.refs_7_) | copy-start | bytes 786436
  30.6 0.9 %copy-start.4 = (bf16[512,256]{1,0:T(8,128)(2,1)S(1)}, bf16[512,256]{1,0:T(8,128)(2,1)}, u32[]{:S(2)}) copy-start(bf16[512,256]{1,0:T(8,128)(2,1)} %constant.12.clone.refs_2_) | copy-start | bytes 786436
  31.6 0.8 %copy-start.5 = (bf16[128,256]{1,0:T(8,128)(2,1)S(1)}, bf16[128,256]{1,0:T(8,128)(2,1)}, u32[]{:S(2)}) copy-start(bf16[128,256]{1,0:T(8,128)(2,1)} %constant.15.clone.refs_5_) | copy-start | bytes 196612
  32.4 0.8 %copy-start.6 = (bf16[128,256]{1,0:T(8,128)(2,1)S(1)}, bf16[128,256]{1,0:T(8,128)(2,1)}, u32[]{:S(2)}) copy-start(bf16[128,256]{1,0:T(8,128)(2,1)} %constant.14.clone.refs_4_) | copy-start | bytes 196612
  33.3 0.8 %copy-start.7 = (bf16[256,128]{1,0:T(8,128)(2,1)S(1)}, bf16[256,128]{1,0:T(8,128)(2,1)}, u32[]{:S(2)}) copy-start(bf16[256,128]{1,0:T(8,128)(2,1)} %constant.13.clone.refs_3_) | copy-start | bytes 196612
  34.1 0.7 %copy-start.8 = (s32[8,8]{1,0:T(8,128)S(1)}, s32[8,8]{1,0:T(8,128)}, u32[]{:S(2)}) copy-start(s32[8,8]{1,0:T(8,128)} %slot_ref.1) | copy-start | bytes 772
  34.8 0.7 %copy-start.9 = (s32[1,3]{1,0:T(1,128)S(1)}, s32[1,3]{1,0:T(1,128)}, u32[]{:S(2)}) copy-start(s32[1,3]{1,0:T(1,128)} %edges_ref.1) | copy-start | bytes 40

commit v4 on v3

--- a/solution.py
+++ b/solution.py
@@ -313,7 +313,7 @@
         ]
         + [pltpu.VMEM(operand.shape, operand.dtype) for operand in operands]
         + [pltpu.SemaphoreType.DMA((8,))],
-        compiler_params=pltpu.CompilerParams(vmem_limit_bytes=40 * 1024 * 1024),
+        compiler_params=pltpu.CompilerParams(vmem_limit_bytes=62 * 1024 * 1024),
     )(edges, slots, *operands)
 
 
@@ -358,6 +358,8 @@
     me = lax.axis_index("segment")
     core = lax.axis_index("template")
     other = {"template": 1 - core}
+    neighbour = me + 1 - 2 * (me % 2)
+    beside = {"segment": neighbour}
 
     def after(step):
         return (me + step) % 8
@@ -397,6 +399,9 @@
         copy.start()
         sends.append(copy)
 
+    for step in (4, 6, 2):
+        begin(remote(block_ref, blocks_out.at[me], 2, step, {"segment": after(step)}))
+    begin(remote(block_ref, blocks_out.at[me], 3, 0, beside))
     for step in FAR_FIRST:
         there = after(step)
         begin(
@@ -408,11 +413,14 @@
                 {"segment": there},
             )
         )
-    for step in FAR_FIRST:
-        begin(remote(block_ref, blocks_out.at[me], 2, step, {"segment": after(step)}))
     begin(remote(own_frame, frames_out.at[core, me], 1, 0, other))
     local_frame.start()
     local_block.start()
+    for step in (2, 6, 4):
+        source = after(8 - step)
+        slot = blocks_out.at[source]
+        remote(slot, slot, 2, step, {"segment": source}).wait_recv()
+        begin(remote(slot, slot, 3, step, beside))
     for step in NEAR_FIRST:
         source = after(8 - step)
         slot = frames_out.at[core, source]
@@ -421,12 +429,11 @@
     local_frame.wait()
     local_block.wait()
     for step in range(8):
-        source = after(8 - step)
-        slot = frames_out.at[1 - core, source]
+        slot = frames_out.at[1 - core, after(8 - step)]
         remote(slot, slot, 1, step, other).wait_recv()
-        if step:
-            slot = blocks_out.at[source]
-            remote(slot, slot, 2, step, {"segment": source}).wait_recv()
+        if step % 2 == 0:
+            slot = blocks_out.at[(neighbour + 8 - step) % 8]
+            remote(slot, slot, 3, step, beside).wait_recv()
     for copy in sends:
         copy.wait_send()
 
@@ -451,8 +458,8 @@
             pltpu.VMEM((9, 16, 1024), BF16),
             pltpu.VMEM((16, WIDE), BF16),
             pltpu.SemaphoreType.DMA((2,)),
-            pltpu.SemaphoreType.DMA((3, 8)),
-            pltpu.SemaphoreType.DMA((3, 8)),
+            pltpu.SemaphoreType.DMA((4, 8)),
+            pltpu.SemaphoreType.DMA((4, 8)),
         ],
         compiler_params=pltpu.CompilerParams(collective_id=0, has_side_effects=True),
     )(strain_frames, templates)

time: 53.2 us -> 42.5 us (0.80)
  local copies, waits for them, and re-layouts: 11.7 us -> 4.28 us
  Pallas kernels: 40.4 us -> 37.3 us
    unnamed x20 -> x0, local copies, waits for them, and re-layouts: 9.43 us -> none
    pallas_call x1, Pallas kernels: 25.4 us -> 21.2 us  [move(): pl.pallas_call(move_kernel, out_shape=(jax.ShapeDtypeStruct((2, 8, 16, 10...]
    reshape x2, local copies, waits for them, and re-layouts: 2.27 us -> 4.28 us  [local(): return (snr.reshape(1, 1, KEPT), chisq.reshape(1, 1, KEPT), peak)]
    pallas_call x1, Pallas kernels: 15 us -> 16.1 us  [compute(): pl.pallas_call(functools.partial(compute_kernel, in_order=in_order), out_...]
where the time goes in v4:
time: 42.5 us; the launch traced here: 42.3 us
  Pallas kernels  37.3 us (88%)
  local copies, waits for them, and re-layouts  4.28 us (10%)
  between operations  0.65 us (2%)
    pallas_call x1, Pallas kernels, move(): pl.pallas_call(move_kernel, out_shape=(jax.ShapeDtypeStruct((2, 8, 16, 10...  21.2 us
    pallas_call x1, Pallas kernels, compute(): pl.pallas_call(functools.partial(compute_kernel, in_order=in_order), out_...  16.1 us
    reshape x2, local copies, waits for them, and re-layouts, local(): return (snr.reshape(1, 1, KEPT), chisq.reshape(1, 1, KEPT), peak)  4.28 us

profile of v4, /device:TPU:0, one launch (start us, length us, event | category | flops | bytes accessed | tf_op | source)
XLA Modules:
  0.0 42.3 jit_solution(6564209977836513409)
XLA Ops:
  0.6 21.2 %shard_map.121 = (bf16[2,8,16,1024]{3,2,1,0:T(8,128)(2,1)}, bf16[8,16,2048]{2,1,0:T(8,128)(2,1)}) custom-call(bf16[8,16384]{1,0:T(8,128)(2,1)} %strain_ref.1, bf16[1,2,16384]{2,1,0:T(2,128)(2,1)} %template_ref.1), custom_call_target="tpu_custom_call" | custom-call | tf_op jit(solution)/shard_map/pallas_call | solution.py:448
  21.9 16.1 %shard_map.122 = (bf16[64,2048]{1,0:T(8,128)(2,1)}, bf16[64,2048]{1,0:T(8,128)(2,1)}, f32[1,1]{1,0:T(1,128)}) custom-call(s32[1,3]{1,0:T(1,128)} %edges_ref.1, s32[8,8]{1,0:T(8,128)} %slot_ref.1, bf16[256,1024]{1,0:T(8,128)(2,1)} %bitcast.2, bf16[128,2048]{1,0:T(8,128)(2,1)} %bitcast.3, bf16[512,256]{1,0:T(8,128)(2,1)} %constant.12.clone.refs_2_, ...), custom_call_target="tpu_custom_call" | custom-call | tf_op jit(solution)/shard_map/pallas_call | solution.py:297
  38.0 2.1 %reshape.20 = bf16[1,1,131072]{2,1,0:T(2,128)(2,1)} reshape(bf16[64,2048]{1,0:T(8,128)(2,1)} %get-tuple-element.10) | data formatting | bytes 524288 | tf_op jit(solution)/shard_map/reshape | solution.py:476
  40.1 2.1 %reshape.21 = bf16[1,1,131072]{2,1,0:T(2,128)(2,1)} reshape(bf16[64,2048]{1,0:T(8,128)(2,1)} %get-tuple-element.11) | data formatting | bytes 524288 | tf_op jit(solution)/shard_map/reshape | solution.py:476

commit v5 on v4

--- a/solution.py
+++ b/solution.py
@@ -280,8 +280,10 @@
             base = (1.0 + reduced * reduced * reduced) * 0.5
             weighted = snr * jnp.exp(jnp.log(base) * (-1.0 / 6.0))
             newsnr = jnp.where(reduced > 1.0, weighted, snr)
-            snr_ref[rows, lanes] = snr.astype(BF16)
-            chisq_ref[rows, lanes] = chisq.astype(BF16)
+            for line in range(16):
+                begin = pl.multiple_of((t * 16 + line) * WIDE + chunk * 512, 512)
+                snr_ref[0, :, pl.ds(begin, 512)] = snr[line : line + 1].astype(BF16)
+                chisq_ref[0, :, pl.ds(begin, 512)] = chisq[line : line + 1].astype(BF16)
             for part in range(4):
                 best = jnp.maximum(best, newsnr[:, part * RADIX_C : (part + 1) * RADIX_C])
         return best
@@ -297,8 +299,8 @@
     return pl.pallas_call(
         functools.partial(compute_kernel, in_order=in_order),
         out_shape=(
-            jax.ShapeDtypeStruct((RADIX_A, WIDE), BF16),
-            jax.ShapeDtypeStruct((RADIX_A, WIDE), BF16),
+            jax.ShapeDtypeStruct((1, 1, KEPT), BF16),
+            jax.ShapeDtypeStruct((1, 1, KEPT), BF16),
             jax.ShapeDtypeStruct((1, 1), F32),
         ),
         in_specs=[smem] * 2 + [pl.BlockSpec(memory_space=pltpu.HBM)] * 8,
@@ -473,7 +475,7 @@
     else:
         segment, template = move_general(strain_frames, frame_slot, templates)
     snr, chisq, peak = compute(bin_edges, frame_slot, segment, template, not direct)
-    return (snr.reshape(1, 1, KEPT), chisq.reshape(1, 1, KEPT), peak)
+    return (snr, chisq, peak)
 
 
 def solution(mesh):

time: 42.5 us -> 38.6 us (0.908)
  local copies, waits for them, and re-layouts: 4.28 us -> 0 us
  Pallas kernels: 37.3 us -> 37.8 us
    reshape x2 -> x0, local copies, waits for them, and re-layouts: 4.28 us -> none  [local(): return (snr.reshape(1, 1, KEPT), chisq.reshape(1, 1, KEPT), peak)]
    pallas_call x1, Pallas kernels: 16.1 us -> 16.6 us  [compute(): pl.pallas_call(functools.partial(compute_kernel, in_order=in_order), out_...]
where the time goes in v5:
time: 38.6 us; the launch traced here: 38.5 us
  Pallas kernels  37.8 us (98%)
  between operations  0.64 us (2%)
    pallas_call x1, Pallas kernels, move(): pl.pallas_call(move_kernel, out_shape=(jax.ShapeDtypeStruct((2, 8, 16, 10...  21.2 us
    pallas_call x1, Pallas kernels, compute(): pl.pallas_call(functools.partial(compute_kernel, in_order=in_order), out_...  16.6 us

profile of v5, /device:TPU:0, one launch (start us, length us, event | category | flops | bytes accessed | tf_op | source)
XLA Modules:
  0.0 38.5 jit_solution(8785374257061848497)
XLA Ops:
  0.6 21.2 %shard_map.121 = (bf16[2,8,16,1024]{3,2,1,0:T(8,128)(2,1)}, bf16[8,16,2048]{2,1,0:T(8,128)(2,1)}) custom-call(bf16[8,16384]{1,0:T(8,128)(2,1)} %strain_ref.1, bf16[1,2,16384]{2,1,0:T(2,128)(2,1)} %template_ref.1), custom_call_target="tpu_custom_call" | custom-call | tf_op jit(solution)/shard_map/pallas_call | solution.py:450
  21.9 16.6 %shard_map.122 = (bf16[1,1,131072]{2,1,0:T(2,128)(2,1)}, bf16[1,1,131072]{2,1,0:T(2,128)(2,1)}, f32[1,1]{1,0:T(1,128)}) custom-call(s32[1,3]{1,0:T(1,128)} %edges_ref.1, s32[8,8]{1,0:T(8,128)} %slot_ref.1, bf16[256,1024]{1,0:T(8,128)(2,1)} %bitcast.2, bf16[128,2048]{1,0:T(8,128)(2,1)} %bitcast.3, bf16[512,256]{1,0:T(8,128)(2,1)} %constant.12.clone.refs_2_, ...), custom_call_target="tpu_custom_call" | custom-call | tf_op jit(solution)/shard_map/pallas_call | solution.py:299

commit v6 on v5

--- a/solution.py
+++ b/solution.py
@@ -375,11 +375,6 @@
     parts = [template_ref[0, :, row * WIDE : (row + 1) * WIDE].astype(F32) for row in range(8)]
     rows = [p[c : c + 1] for c in range(2) for p in parts]
     block_ref[...] = jnp.concatenate(rows, axis=0).astype(BF16)
-    for row in range(16):
-        wide_ref[:, row, :] = strain_ref[:, row * 1024 : (row + 1) * 1024].astype(F32)
-    for frame in range(8):
-        frames_ref[frame] = wide_ref[frame].astype(BF16)
-    frames_ref[8] = jnp.zeros((16, 1024), BF16)
     pl.semaphore_wait(barrier, 8)
 
     def remote(source, target, row, step, device):
@@ -404,6 +399,11 @@
     for step in (4, 6, 2):
         begin(remote(block_ref, blocks_out.at[me], 2, step, {"segment": after(step)}))
     begin(remote(block_ref, blocks_out.at[me], 3, 0, beside))
+    for row in range(16):
+        wide_ref[:, row, :] = strain_ref[:, row * 1024 : (row + 1) * 1024].astype(F32)
+    for frame in range(8):
+        frames_ref[frame] = wide_ref[frame].astype(BF16)
+    frames_ref[8] = jnp.zeros((16, 1024), BF16)
     for step in FAR_FIRST:
         there = after(step)
         begin(

time: 38.6 us -> 38.6 us (level)
  no operation moved by 1% of the time
where the time goes in v6:
time: 38.6 us; the launch traced here: 38.5 us
  Pallas kernels  37.8 us (98%)
  between operations  0.64 us (2%)
    pallas_call x1, Pallas kernels, move(): pl.pallas_call(move_kernel, out_shape=(jax.ShapeDtypeStruct((2, 8, 16, 10...  21.2 us
    pallas_call x1, Pallas kernels, compute(): pl.pallas_call(functools.partial(compute_kernel, in_order=in_order), out_...  16.6 us

profile of v6, /device:TPU:0, one launch (start us, length us, event | category | flops | bytes accessed | tf_op | source)
XLA Modules:
  0.0 38.5 jit_solution(1053587694189095642)
XLA Ops:
  0.6 21.2 %shard_map.121 = (bf16[2,8,16,1024]{3,2,1,0:T(8,128)(2,1)}, bf16[8,16,2048]{2,1,0:T(8,128)(2,1)}) custom-call(bf16[8,16384]{1,0:T(8,128)(2,1)} %strain_ref.1, bf16[1,2,16384]{2,1,0:T(2,128)(2,1)} %template_ref.1), custom_call_target="tpu_custom_call" | custom-call | tf_op jit(solution)/shard_map/pallas_call | solution.py:450
  21.9 16.6 %shard_map.122 = (bf16[1,1,131072]{2,1,0:T(2,128)(2,1)}, bf16[1,1,131072]{2,1,0:T(2,128)(2,1)}, f32[1,1]{1,0:T(1,128)}) custom-call(s32[1,3]{1,0:T(1,128)} %edges_ref.1, s32[8,8]{1,0:T(8,128)} %slot_ref.1, bf16[256,1024]{1,0:T(8,128)(2,1)} %bitcast.2, bf16[128,2048]{1,0:T(8,128)(2,1)} %bitcast.3, bf16[512,256]{1,0:T(8,128)(2,1)} %constant.12.clone.refs_2_, ...), custom_call_target="tpu_custom_call" | custom-call | tf_op jit(solution)/shard_map/pallas_call | solution.py:299
